TPU v7x, 512 devices: a whole 4x8x8 slice. The times are simulated.
512 devices in a mesh: dp: 16 (over z, y_hi), space: 32 (over x, y_lo, core).
Axes of the slice: x: 4, y: 8 (y_hi: 2, y_lo: 4; y = y_hi * 4 + y_lo), z: 8, core: 2. Of those that a mesh axis runs over, the one named last changes fastest.
Arguments:
- volume: bfloat16 [16, 4, 256, 8, 256], P('dp', None, 'space'), may hold values from -6 to 6
- first_weight: bfloat16 [32, 108], replicated, may hold values from -0.625 to 0.625
- first_bias: float32 [32], replicated, may hold values from -3 to 3
- second_weight: bfloat16 [64, 864], replicated, may hold values from -0.21875 to 0.21875
- second_bias: float32 [64], replicated, may hold values from -3 to 3
- cotangent: bfloat16 [16, 64, 128, 4, 128], P('dp', None, 'space'), may hold values from -6 to 6
Outputs:
- activation: bfloat16 [16, 64, 128, 4, 128], P('dp', None, 'space')
- grad_first_weight: float32 [32, 108], replicated
- grad_first_bias: float32 [32], replicated
- grad_second_weight: float32 [64, 864], replicated
- grad_second_bias: float32 [64], replicated
All inputs are finite; a program needn't handle non-finite values.
Results may differ from a plain program's by a relative error of at most 0.011.
The roundings to bfloat16 on the way count: a program that leaves them out, or rounds other values in their place, can miss the bound.
Values may be sent and summed in bfloat16 or wider, within the bound.
No kernel may reach another device: no remote copies, remote signals or barrier semaphores. Data moves between devices by JAX's collectives and lax.ppermute only.
A program may use at most 128 MiB of HBM per device.

v0:
```python
import math

import jax
import jax.numpy as jnp
from jax import lax
from jax.sharding import PartitionSpec as P

leak_slope = 0.3


def with_halo(block, sides, width):
    for axis, dim in sides:
        count = lax.axis_size(axis)
        forward = [(i, i + 1) for i in range(count - 1)]
        backward = [(target, source) for source, target in forward]
        low = lax.ppermute(
            lax.slice_in_dim(block, block.shape[dim] - width, None, axis=dim), axis, forward
        )
        high = lax.ppermute(lax.slice_in_dim(block, 0, width, axis=dim), axis, backward)
        block = jnp.concatenate([low, block, high], axis=dim)
    return block


def columns(padded, planes, height, depth):
    shifted = []
    for along_p in range(3):
        for along_y in range(3):
            for along_z in range(3):
                shifted.append(
                    padded[
                        :,
                        along_p : along_p + planes,
                        along_y : along_y + height,
                        along_z : along_z + depth,
                    ]
                )
    stacked = jnp.stack(shifted, 0)
    return stacked.reshape(27 * padded.shape[0], planes * height * depth)


def avg_pool(field):
    chans, planes, height, depth = field.shape
    return field.reshape(chans, planes // 2, 2, height // 2, 2, depth // 2, 2).mean(axis=(2, 4, 6))


def unpool(grad):
    chans, planes, height, depth = grad.shape
    spread = jnp.broadcast_to(
        grad[:, :, None, :, None, :, None], (chans, planes, 2, height, 2, depth, 2)
    )
    return spread.reshape(chans, -1) * 0.125


def pad_sides(field):
    return jnp.pad(field, ((0, 0), (0, 0), (1, 1), (1, 1)))


def on_device(volume, first_weight, first_bias, second_weight, second_bias, cotangent):
    filters_one = first_weight.shape[0]
    filters_two = second_weight.shape[0]
    planes, height, depth = (volume.shape[2], volume.shape[3], volume.shape[4])
    half_p, half_y, half_z = (planes // 2, height // 2, depth // 2)
    dims = (((1,), (1,)), ((), ()))
    extended = with_halo(volume, (("space", 2),), 1)[0]
    stacked_first = columns(pad_sides(extended), planes, height, depth)
    pre_first = (
        jnp.dot(first_weight, stacked_first, preferred_element_type=jnp.float32)
        + first_bias[:, None]
    )
    act_first = jnp.where(pre_first > 0, pre_first, leak_slope * pre_first)
    pooled = avg_pool(act_first.reshape(filters_one, planes, height, depth)).astype(jnp.bfloat16)
    pooled_ext = with_halo(pooled[None], (("space", 2),), 1)[0]
    stacked_second = columns(pad_sides(pooled_ext), half_p, half_y, half_z)
    pre_second = (
        jnp.dot(second_weight, stacked_second, preferred_element_type=jnp.float32)
        + second_bias[:, None]
    )
    activation = jnp.where(pre_second > 0, pre_second, leak_slope * pre_second).astype(jnp.bfloat16)
    slope_second = jnp.where(pre_second > 0, 1.0, leak_slope)
    grad_pre_second = (
        cotangent[0].reshape(filters_two, -1).astype(jnp.float32) * slope_second
    ).astype(jnp.bfloat16)
    grad_second_weight = lax.dot_general(
        grad_pre_second, stacked_second, dims, preferred_element_type=jnp.float32
    )
    grad_second_bias = jnp.sum(grad_pre_second.astype(jnp.float32), axis=1)
    grad_field = grad_pre_second.reshape(filters_two, half_p, half_y, half_z)
    flipped = (
        second_weight.reshape(filters_two, 27, filters_one)[:, ::-1, :]
        .transpose(2, 1, 0)
        .reshape(filters_one, 27 * filters_two)
    )
    grad_ext = with_halo(grad_field[None], (("space", 2),), 1)[0]
    stacked_back = columns(pad_sides(grad_ext), half_p, half_y, half_z)
    grad_pooled = jnp.dot(flipped, stacked_back, preferred_element_type=jnp.float32)
    slope_first = jnp.where(pre_first > 0, 1.0, leak_slope)
    grad_pre_first = (
        unpool(grad_pooled.reshape(filters_one, half_p, half_y, half_z)) * slope_first
    ).astype(jnp.bfloat16)
    grad_first_weight = lax.dot_general(
        grad_pre_first, stacked_first, dims, preferred_element_type=jnp.float32
    )
    grad_first_bias = jnp.sum(grad_pre_first.astype(jnp.float32), axis=1)
    grad_first_weight, grad_first_bias, grad_second_weight, grad_second_bias = lax.psum(
        (grad_first_weight, grad_first_bias, grad_second_weight, grad_second_bias), ("dp", "space")
    )
    count_first = float(planes * height * depth * lax.axis_size("dp") * lax.axis_size("space"))
    scale_first = 1.0 / math.sqrt(count_first)
    scale_second = 1.0 / math.sqrt(count_first / 8.0)
    activation = activation.reshape(1, filters_two, half_p, half_y, half_z)
    return (
        activation,
        grad_first_weight * scale_first,
        grad_first_bias * scale_first,
        grad_second_weight * scale_second,
        grad_second_bias * scale_second,
    )


def solution(mesh):
    return jax.shard_map(
        on_device,
        mesh=mesh,
        in_specs=(
            P("dp", None, "space", None, None),
            P(),
            P(),
            P(),
            P(),
            P("dp", None, "space", None, None),
        ),
        out_specs=(P("dp", None, "space", None, None), P(), P(), P(), P()),
        check_vma=False,
    )
```

profile of v0, /device:TPU:1, one launch (start us, length us, event | category | flops | bytes accessed | tf_op | source)
XLA Modules:
  0.0 363.4 jit_solution(13507432957899154006)
XLA Ops:
  8.0 4.6 %collective-permute-start = (bf16[1,4,1,8,256]{4,3,2,1,0:T(8,128)(2,1)S(1)}, bf16[1,4,1,8,256]{4,3,2,1,0:T(8,128)(2,1)S(1)}, u32[]{:S(2)}, u32[]{:S(2)}) collective-permute-start(bf16[1,4,1,8,256]{4,3,2,1,0:T(8,128)(2,1)S(1)} %get-tuple-element.17), channel_id=1, source_target_pairs={{0,1},{1,2},{2,3},{3,4},{4,5},{5,6},{6,7},{7,8},{8,9},{9,10},{10,1... | collective-permute-start | bytes 49160 | tf_op jit(solution)/shard_map/ppermute | solution.py:16
  12.6 5.5 %collective-permute-start.1 = (bf16[1,4,1,8,256]{4,3,2,1,0:T(8,128)(2,1)S(1)}, bf16[1,4,1,8,256]{4,3,2,1,0:T(8,128)(2,1)S(1)}, u32[]{:S(2)}, u32[]{:S(2)}) collective-permute-start(bf16[1,4,1,8,256]{4,3,2,1,0:T(8,128)(2,1)S(1)} %get-tuple-element.18), channel_id=1, source_target_pairs={{1,0},{2,1},{3,2},{4,3},{5,4},{6,5},{7,6},{8,7},{9,8},{10,9},{11,1... | collective-permute-start | bytes 49160 | tf_op jit(solution)/shard_map/ppermute | solution.py:19
  18.0 1.7 copy.32
  19.8 0.9 maximum_bitcast_fusion.2
  23.2 3.5 reshape.51
  26.6 4.0 %multiply_select_fusion = (f32[32,16384]{1,0:T(8,128)S(1)}, f32[32,16384]{1,0:T(8,128)}) fusion(f32[32]{0:T(128)S(1)} %copy-done.6, bf16[108,16384]{1,0:T(8,128)(2,1)} %reshape.51, bf16[32,108]{1,0:T(8,128)(2,1)S(1)} %copy-done), kind=kOutput, calls=%fused_computation.50 | convolution fusion | flops 115343360 | bytes 7740288 | tf_op jit(solution)/shard_map/dot_general | solution.py:67
  30.7 4.7 %copy.27 = f32[32,16384]{0,1:T(8,128)} copy(f32[32,16384]{1,0:T(8,128)S(1)} %get-tuple-element.19) | data formatting | bytes 4194304 | tf_op jit(solution)/shard_map/jit(_where)/select_n | solution.py:70
  35.3 8.8 %reduce_sum.27 = f32[32,4,4,128]{0,3,2,1:T(8,128)S(1)} reduce(f32[32,4,2,4,2,128,2]{0,6,5,4,3,2,1:T(2,128)} %bitcast.356, f32[]{:T(128)} %constant.8.clone.1), dimensions={2,4,6}, to_apply=%region_0.1 | reduce | flops 458752 | bytes 2359300 | tf_op jit(solution)/shard_map/reduce_sum | solution.py:43
  44.3 1.9 collective-permute-start.2
  46.2 2.6 collective-permute-start.3
  48.9 0.9 reshape.57
  51.1 2.7 collective-permute-done.3
  56.5 3.6 copy.31
  60.0 5.6 %reshape.52 = bf16[864,2048]{1,0:T(8,128)(2,1)S(1)} reshape(bf16[27,32,4,4,128]{4,3,2,1,0:T(4,128)(2,1)} %copy.31) | data formatting | bytes 7077888 | tf_op jit(solution)/shard_map/reshape | solution.py:38
  65.7 2.8 convert_reduce_fusion.1
  68.5 1.8 broadcast_in_dim_reshape.4
  70.4 1.6 fusion.111
  71.9 1.9 collective-permute-start.4
  73.8 3.2 collective-permute-start.5
  77.1 2.8 fusion.114
  79.9 1.8 reshape.53
  81.8 1.3 maximum_bitcast_fusion
  83.0 1.0 fusion.10
  84.9 1.0 fusion.14
  87.6 1.0 fusion.18
  88.6 1.0 fusion.20
  90.5 1.0 fusion.24
  91.5 1.0 fusion.26
  93.3 1.0 fusion.30
  94.3 0.9 fusion.32
  96.0 0.9 fusion.34
  97.0 1.0 fusion.36
  98.8 1.0 fusion.40
  99.8 1.0 fusion.42
  101.6 1.0 fusion.46
  102.6 0.9 fusion.48
  104.3 0.9 fusion.50
  105.3 1.0 fusion.52
  107.1 1.0 fusion.56
  108.1 12.4 %reshape.54 = bf16[1728,2048]{1,0:T(8,128)(2,1)} reshape(bf16[27,64,4,4,128]{4,3,2,1,0:T(4,128)(2,1)} %fusion.56) | data formatting | bytes 14155776 | tf_op jit(solution)/shard_map/reshape | solution.py:38
  120.6 4.4 %fusion.2 = f32[32,2048]{1,0:T(8,128)S(1)} fusion(bf16[32,1728]{1,0:T(8,128)(2,1)S(1)} %copy-done.3, bf16[1728,2048]{1,0:T(8,128)(2,1)} %reshape.54), kind=kOutput, calls=%fused_computation.79 | convolution fusion | flops 226557952 | bytes 7450624 | tf_op jit(solution)/shard_map/dot_general | solution.py:95
  125.3 7.3 %broadcast_in_dim.21 = f32[32,4,2,4,2,128,2]{0,6,5,4,3,2,1:T(2,128)} broadcast(f32[32,4,4,128]{0,3,2,1:T(8,128)S(1)} %bitcast.358), dimensions={0,1,3,5} | broadcast | bytes 2359296 | tf_op jit(solution)/shard_map/broadcast_in_dim | solution.py:48
  132.6 6.4 %copy.35 = f32[32,16384]{1,0:T(8,128)} copy(f32[32,16384]{0,1:T(8,128)} %bitcast.357) | data formatting | bytes 4194304 | tf_op jit(solution)/shard_map/mul | solution.py:51
  139.1 2.3 convert_reduce_fusion
  141.8 1.4 fusion.113
  143.1 109.8 %all-reduce.3 = (f32[32,108]{1,0:T(8,128)S(1)}, f32[32]{0:T(128)S(1)}, f32[64]{0:T(128)S(1)}) all-reduce(f32[32,108]{1,0:T(8,128)S(1)} %fusion.113, f32[32]{0:T(128)S(1)} %get-tuple-element.10, f32[64]{0:T(128)S(1)} %get-tuple-element.8), channel_id=1, replica_groups=mesh['dp'=16,'space'=32] {'dp','space'}, use_global_device_ids=true, to_apply=%region_1.2 | all-reduce | flops 3552 | bytes 28416 | tf_op jit(solution)/shard_map/psum | solution.py:104
  254.6 100.3 %all-reduce.6.cloned.1.call-done = f32[64,864]{1,0:T(8,128)} async-done(((f32[64,864]{1,0:T(8,128)}), f32[64,864]{1,0:T(8,128)}) %all-reduce.6.cloned.1.call-update) | async-done | bytes 221200 | tf_op jit(solution)/shard_map/psum | solution.py:104
  354.9 1.6 broadcast_multiply_fusion
  (101 shorter events, 17.9 us)
Async XLA Ops:
  7.2 19.5 %copy-start = (bf16[32,108]{1,0:T(8,128)(2,1)S(1)}, bf16[32,108]{1,0:T(8,128)(2,1)}, u32[]{:S(2)}) copy-start(bf16[32,108]{1,0:T(8,128)(2,1)} %param.7) | copy-start | bytes 20740
  7.2 347.8 %all-reduce.6.cloned.1.call-start = ((), (), s32[]{:S(2)}) async-start(), calls=%async_computation | async-start | bytes 458752 | tf_op jit(solution)/shard_map/psum | solution.py:104
  8.0 11.8 %collective-permute-start = (bf16[1,4,1,8,256]{4,3,2,1,0:T(8,128)(2,1)S(1)}, bf16[1,4,1,8,256]{4,3,2,1,0:T(8,128)(2,1)S(1)}, u32[]{:S(2)}, u32[]{:S(2)}) collective-permute-start(bf16[1,4,1,8,256]{4,3,2,1,0:T(8,128)(2,1)S(1)} %get-tuple-element.17), channel_id=1, source_target_pairs={{0,1},{1,2},{2,3},{3,4},{4,5},{5,6},{6,7},{7,8},{8,9},{9,10},{10,1... | collective-permute-start | bytes 49160 | tf_op jit(solution)/shard_map/ppermute | solution.py:16
  12.6 7.2 %collective-permute-start.1 = (bf16[1,4,1,8,256]{4,3,2,1,0:T(8,128)(2,1)S(1)}, bf16[1,4,1,8,256]{4,3,2,1,0:T(8,128)(2,1)S(1)}, u32[]{:S(2)}, u32[]{:S(2)}) collective-permute-start(bf16[1,4,1,8,256]{4,3,2,1,0:T(8,128)(2,1)S(1)} %get-tuple-element.18), channel_id=1, source_target_pairs={{1,0},{2,1},{3,2},{4,3},{5,4},{6,5},{7,6},{8,7},{9,8},{10,9},{11,1... | collective-permute-start | bytes 49160 | tf_op jit(solution)/shard_map/ppermute | solution.py:19
  23.2 3.5 copy-start.6
  35.3 13.5 %copy-start.4 = (bf16[64,864]{0,1:T(8,128)(2,1)S(1)}, bf16[64,864]{0,1:T(8,128)(2,1)}, u32[]{:S(2)}) copy-start(bf16[64,864]{0,1:T(8,128)(2,1)} %copy.32) | copy-start | bytes 331780
  35.3 13.5 %copy-start.5 = (bf16[1,64,4,4,128]{4,3,2,1,0:T(4,128)(2,1)S(1)}, bf16[1,64,4,4,128]{4,3,2,1,0:T(4,128)(2,1)}, u32[]{:S(2)}) copy-start(bf16[1,64,4,4,128]{4,3,2,1,0:T(4,128)(2,1)} %param.11) | copy-start | bytes 786436
  44.3 6.7 %collective-permute-start.2 = (bf16[1,32,1,4,128]{1,4,3,2,0:T(8,128)(2,1)S(1)}, bf16[1,32,1,4,128]{1,4,3,2,0:T(8,128)(2,1)S(1)}, u32[]{:S(2)}, u32[]{:S(2)}) collective-permute-start(bf16[1,32,1,4,128]{1,4,3,2,0:T(8,128)(2,1)S(1)} %get-tuple-element.13), channel_id=1, source_target_pairs={{0,1},{1,2},{2,3},{3,4},{4,5},{5,6},{6,7},{7,8},{8,9},{9,10},{10,1... | collective-permute-start | bytes 98312 | tf_op jit(solution)/shard_map/ppermute | solution.py:16
  46.2 7.6 %collective-permute-start.3 = (bf16[1,32,1,4,128]{1,4,3,2,0:T(8,128)(2,1)S(1)}, bf16[1,32,1,4,128]{1,4,3,2,0:T(8,128)(2,1)S(1)}, u32[]{:S(2)}, u32[]{:S(2)}) collective-permute-start(bf16[1,32,1,4,128]{1,4,3,2,0:T(8,128)(2,1)S(1)} %get-tuple-element.14), channel_id=1, source_target_pairs={{1,0},{2,1},{3,2},{4,3},{5,4},{6,5},{7,6},{8,7},{9,8},{10,9},{11,1... | collective-permute-start | bytes 98312 | tf_op jit(solution)/shard_map/ppermute | solution.py:19
  60.0 5.6 %copy-start.7 = (f32[64]{0:T(128)S(1)}, f32[64]{0:T(128)}, u32[]{:S(2)}) copy-start(f32[64]{0:T(128)} %param.10) | copy-start | bytes 772
  71.9 9.8 %collective-permute-start.4 = (bf16[1,64,1,4,128]{4,3,2,1,0:T(4,128)(2,1)}, bf16[1,64,1,4,128]{4,3,2,1,0:T(4,128)(2,1)}, u32[]{:S(2)}, u32[]{:S(2)}) collective-permute-start(bf16[1,64,1,4,128]{4,3,2,1,0:T(4,128)(2,1)} %get-tuple-element.15), channel_id=1, source_target_pairs={{0,1},{1,2},{2,3},{3,4},{4,5},{5,6},{6,7},{7,8},{8,9},{9,10},{10,1... | collective-permute-start | bytes 196616 | tf_op jit(solution)/shard_map/ppermute | solution.py:16
  73.8 7.9 %collective-permute-start.5 = (bf16[1,64,1,4,128]{4,3,2,1,0:T(4,128)(2,1)}, bf16[1,64,1,4,128]{4,3,2,1,0:T(4,128)(2,1)}, u32[]{:S(2)}, u32[]{:S(2)}) collective-permute-start(bf16[1,64,1,4,128]{4,3,2,1,0:T(4,128)(2,1)} %get-tuple-element.16), channel_id=1, source_target_pairs={{1,0},{2,1},{3,2},{4,3},{5,4},{6,5},{7,6},{8,7},{9,8},{10,9},{11,1... | collective-permute-start | bytes 196616 | tf_op jit(solution)/shard_map/ppermute | solution.py:19
  108.1 12.4 %copy-start.3 = (bf16[32,1728]{1,0:T(8,128)(2,1)S(1)}, bf16[32,1728]{1,0:T(8,128)(2,1)}, u32[]{:S(2)}) copy-start(bf16[32,1728]{1,0:T(8,128)(2,1)} %reshape.56) | copy-start | bytes 331780
  132.6 6.5 %copy-start.2 = (f32[32,16384]{1,0:T(8,128)S(1)}, f32[32,16384]{1,0:T(8,128)}, u32[]{:S(2)}) copy-start(f32[32,16384]{1,0:T(8,128)} %get-tuple-element.20) | copy-start | bytes 6291460
  139.1 2.7 copy-start.1
Sparse Core Ops, SparseCore 0:
  80.0 274.8 all-reduce.5
where the time goes:
time: 364 us; the launch traced here: 363 us
  blocking collectives  110 us (30%)
  waiting for transfers between devices  103 us (28%)
  local copies, waits for them, and re-layouts  84 us (23%)
  starting transfers between devices  19.7 us (5%)
  other arithmetic  16.8 us (5%)
  matrix products  15.5 us (4%)
  between operations  14.6 us (4%)
    psum x1, blocking collectives, on_device(): lax.psum((grad_first_weight, grad_first_bias, grad_second_weight, grad_se...  110 us
    psum x1, waiting for transfers between devices, on_device(): lax.psum((grad_first_weight, grad_first_bias, grad_second_weight, grad_se...  100 us
    unnamed x95, local copies, waits for them, and re-layouts  30.6 us
    reshape x3, local copies, waits for them, and re-layouts, columns(): return stacked.reshape(27 * padded.shape[0], planes * height * depth)  21.5 us
    ppermute x3, starting transfers between devices, with_halo(): lax.ppermute(lax.slice_in_dim(block, 0, width, axis=dim), axis, backward)  11.3 us
    reduce_sum x1, other arithmetic, avg_pool(): field.reshape(chans, planes // 2, 2, height // 2, 2, depth // 2, 2)  8.83 us
    ppermute x3, starting transfers between devices, with_halo(): lax.ppermute(lax.slice_in_dim(block, block.shape[dim] - width, None, axis...  8.41 us
    broadcast_in_dim x1, local copies, waits for them, and re-layouts, unpool(): jnp.broadcast_to(grad[:, :, None, :, None, :, None], (chans, planes, 2, h...  7.31 us
  transfers between devices with their start and end apart: 7, of which 2 were waited for; matrix products, arithmetic and copies ran while one was open for 20% of the time, Pallas kernels for 0%

commit v1 on v0

v1 whole, which is shorter than its diff:
```python
import math

import jax
import jax.numpy as jnp
import numpy as np
from jax import lax
from jax.experimental import pallas as pl
from jax.experimental.pallas import tpu as pltpu
from jax.sharding import Mesh, PartitionSpec as P

leak_slope = 0.3
F32, BF16 = jnp.float32, jnp.bfloat16
HALO = 5
NT = (((1,), (1,)), ((), ()))


def split_matrix():
    d = np.zeros((256, 4, 128), np.float32)
    for dz in range(4):
        for k in range(128):
            z = 2 * k - 1 + dz
            if 0 <= z < 256:
                d[z, dz, k] = 1.0
    return d.reshape(256, 512)


def spread_matrix():
    sel = np.zeros((27, 4, 8, 4, 4, 4, 4), np.float32)
    for s in range(8):
        sz, sx, sy = s // 4, s // 2 % 2, s % 2
        for t in range(27):
            tx, ty, tz = t // 9, t // 3 % 3, t % 3
            for c in range(4):
                sel[t, c, s, tx + sx, ty + sy, tz + sz, c] = 1.0
    return sel.reshape(108, 2048)


def compact_matrix():
    m = np.zeros((256, 128), np.float32)
    for g in range(9):
        for j in range(12):
            m[g * 16 + j, g * 12 + j] = 1.0
    return m


def prepare_kernel(w1_ref, w2_ref, sel_ref, w1big_ref, wexp_ref, wt_ref, w2_pad):
    for s in range(8):
        w1big_ref[s * 32 : (s + 1) * 32, :] = jnp.dot(
            w1_ref[...], sel_ref[:, s * 256 : (s + 1) * 256], preferred_element_type=F32
        ).astype(BF16)
    w2_pad[:, 768:1024] = jnp.zeros((64, 256), F32)
    w2_pad[:, 0:864] = w2_ref[...].astype(F32)
    lane = lax.broadcasted_iota(jnp.int32, (64, 128), 1)
    zero = jnp.zeros((64, 128), F32)
    units = []
    for u in range(9):
        start = 96 * u // 128 * 128
        window = w2_pad[:, start : start + 256]
        if 96 * u > start:
            window = pltpu.roll(window, 256 - (96 * u - start), 1)
        units.append(jnp.where(lane < 96, window[:, :128], 0.0))
    for dx in range(3):
        for yin in range(4):
            at = (dx * 4 + yin) * 128
            rows = []
            for y in range(4):
                dy = yin - y + 1
                rows.append(units[dx * 3 + dy] if 0 <= dy <= 2 else zero)
            for pair in range(2):
                block = jnp.concatenate(rows[2 * pair : 2 * pair + 2], axis=0)
                wexp_ref[pair * 128 : (pair + 1) * 128, at : at + 128] = block.astype(BF16)
                col = (2 - dx) * 256 + pair * 128
                wt_ref[yin * 96 : (yin + 1) * 96, col : col + 128] = block.T[:96].astype(BF16)


def main_kernel(
    place_ref, vol_ref, vlo_ref, vhi_ref, cot_ref, clo_ref, chi_ref, split_ref, compact_ref,
    w1_ref, b1_ref, wexp_ref, b2_ref, wt_ref,
    act_ref, grad_ref,
    fine, win, ps, g2s, pre_s,
    *, scale_first, scale_second,
):
    place = place_ref[0]
    last = place_ref[1]
    x0 = 0
    for ref, count in ((vlo_ref, HALO), (vol_ref, 8), (vhi_ref, HALO)):
        rows = ref[...].astype(F32).reshape(4 * count * 8, 256).astype(BF16)
        parts = jnp.dot(rows, split_ref[...], preferred_element_type=F32)
        for c in range(4):
            for x in range(count):
                for dz in range(4):
                    fine[pl.ds((x0 + x) * 128 + dz * 32 + c * 8, 8), :] = parts[
                        (c * count + x) * 8 : (c * count + x + 1) * 8, dz * 128 : (dz + 1) * 128
                    ]
        x0 += count
    for x in range(8 + 2 * HALO):
        win[x, 0:16, :] = jnp.zeros((16, 128), BF16)
        win[x, 144:160, :] = jnp.zeros((16, 128), BF16)
        for y in range(8):
            win[x, (y + 1) * 16 : (y + 2) * 16, :] = fine[pl.ds(x * 128 + y, 16, stride=8), :].astype(BF16)

    def window(q, y):
        return jnp.concatenate([win[2 * q + dx, 32 * y : 32 * y + 64, :] for dx in range(4)], axis=0)

    lane = lax.broadcasted_iota(jnp.int32, (32, 128), 1)
    bias1 = b1_ref[...]
    bias1 = jnp.concatenate([bias1, bias1], axis=1)
    bias2 = b2_ref[...]
    bias2 = jnp.concatenate([bias2, bias2], axis=1)
    ones = jnp.ones((32, 128), BF16)
    for q in range(8):
        for yp in range(2):
            y0 = 2 * yp
            both = jnp.concatenate([window(q, y0), window(q, y0 + 1)], axis=1)
            pre = jnp.dot(w1_ref[...], both, preferred_element_type=F32) + bias1
            if 2 <= q < 6:
                for i in range(2):
                    pre_s[(q - 2) * 4 + y0 + i] = pre[:, i * 128 : (i + 1) * 128].astype(BF16)
            act = jnp.maximum(pre, leak_slope * pre)
            total = act[0:32]
            for s in range(1, 8):
                total = total + act[s * 32 : (s + 1) * 32]
            total = total * 0.125
            if q < 2:
                total = jnp.where(place > 0, total, 0.0)
            if q >= 6:
                total = jnp.where(place < last, total, 0.0)
            for i in range(2):
                pooled = total[:, i * 128 : (i + 1) * 128]
                at = q * 512 + (y0 + i) * 128
                ps[at : at + 32, :] = jnp.where(lane == 0, 0.0, pltpu.roll(pooled, 1, 1)).astype(BF16)
                ps[at + 32 : at + 64, :] = pooled.astype(BF16)
                ps[at + 64 : at + 96, :] = jnp.where(lane == 127, 0.0, pltpu.roll(pooled, 127, 1)).astype(BF16)
                ps[at + 96 : at + 128, :] = ones

    for r0 in range(0, 6, 2):
        both = jnp.concatenate([ps[r * 512 : (r + 3) * 512, :] for r in (r0, r0 + 1)], axis=1)
        pre = jnp.dot(wexp_ref[...], both, preferred_element_type=F32) + bias2
        act = jnp.maximum(pre, leak_slope * pre)
        for i in range(2):
            r = r0 + i
            cot = (clo_ref[...] if r == 0 else chi_ref[...] if r == 5 else cot_ref[r - 1]).astype(F32)
            own = pre[:, i * 128 : (i + 1) * 128]
            g2s[r * 256 : (r + 1) * 256, :] = jnp.where(own > 0, cot, leak_slope * cot).astype(BF16)
            if 1 <= r <= 4:
                act_ref[r - 1] = act[:, i * 128 : (i + 1) * 128].astype(BF16)

    lane96 = lax.broadcasted_iota(jnp.int32, (96, 128), 1)
    grads = jnp.concatenate([g2s[(p + 1) * 256 : (p + 2) * 256, :] for p in range(4)], axis=1)
    folded = []
    b2_grad = None
    for dx in range(3):
        cols = jnp.concatenate([ps[(p + 1 + dx) * 512 : (p + 2 + dx) * 512, :] for p in range(4)], axis=1)
        t = lax.dot_general(cols, grads, NT, preferred_element_type=F32)
        if dx == 0:
            b2_grad = t[96:104, 0:128] + t[96:104, 128:256]
        for dy in range(3):
            sums = []
            for parity in range(2):
                total = None
                for y in (parity, parity + 2):
                    yin = y + dy - 1
                    if 0 <= yin < 4:
                        piece = t[yin * 128 : yin * 128 + 96, (y // 2) * 128 : (y // 2 + 1) * 128]
                        total = piece if total is None else total + piece
                sums.append(total)
            u = jnp.where(lane96 < 64, sums[0], sums[1])
            folded.append(u + pltpu.roll(u, 64, 1))
    folded = jnp.concatenate(folded + [jnp.zeros((160, 128), F32)], axis=0) * scale_second
    lane128 = lax.broadcasted_iota(jnp.int32, (128, 128), 1)
    for j in range(0, 8, 2):
        two = jnp.where(lane128 < 64, folded[j * 128 : (j + 1) * 128], folded[(j + 1) * 128 : (j + 2) * 128]).T
        grad_ref[j] = two[:64]
        if j < 6:
            grad_ref[j + 1] = two[64:]

    ones16 = jnp.ones((16, 512), BF16)
    m1 = None
    for pp in range(2):
        q = jnp.dot(
            wt_ref[...],
            jnp.concatenate([g2s[p * 256 : (p + 3) * 256, :] for p in (2 * pp, 2 * pp + 1)], axis=1),
            preferred_element_type=F32,
        )
        for i in range(2):
            p = 2 * pp + i
            cells = []
            for y in range(4):
                three = q[y * 96 : (y + 1) * 96, i * 128 : (i + 1) * 128] * 0.125
                g = (
                    jnp.where(lane == 127, 0.0, pltpu.roll(three[0:32], 127, 1))
                    + three[32:64]
                    + jnp.where(lane == 0, 0.0, pltpu.roll(three[64:96], 1, 1))
                )
                low = leak_slope * g
                pre = pre_s[p * 4 + y].astype(F32)
                cells.append(
                    jnp.concatenate(
                        [jnp.where(pre[s * 32 : (s + 1) * 32] > 0, g, low) for s in range(8)], axis=0
                    ).astype(BF16)
                )
            cols = jnp.concatenate([window(p + 2, y) for y in range(4)], axis=1)
            cols = jnp.concatenate([cols, ones16], axis=0)
            t = lax.dot_general(cols, jnp.concatenate(cells, axis=1), NT, preferred_element_type=F32)
            m1 = t if m1 is None else m1 + t

    lane16 = lax.broadcasted_iota(jnp.int32, (16, 128), 1)
    half = []
    for g in range(16):
        half.append(m1[g * 16 : (g + 1) * 16, 0:128] + pltpu.roll(m1[g * 16 : (g + 1) * 16, 128:256], 12, 0))
    groups = []
    for tx in range(3):
        for ty in range(3):
            a = half[tx * 4 + ty]
            b = half[tx * 4 + ty + 1]
            c = half[(tx + 1) * 4 + ty]
            d = half[(tx + 1) * 4 + ty + 1]
            v = jnp.where(lane16 < 32, a, jnp.where(lane16 < 64, b, jnp.where(lane16 < 96, c, d)))
            v = v + pltpu.roll(v, 64, 1)
            groups.append(v + pltpu.roll(v, 32, 1))
    first = jnp.concatenate(groups[:8], axis=0).T[:32]
    ninth = jnp.concatenate([groups[8], jnp.zeros((112, 128), F32)], axis=0).T[:32]
    w1_grad = jnp.dot(
        jnp.concatenate([first, ninth], axis=1),
        compact_ref[...],
        precision=lax.Precision.HIGHEST,
        preferred_element_type=F32,
    )
    b1_grad = m1[256:264, 0:128] + m1[256:264, 128:256]
    b1_grad = b1_grad + pltpu.roll(b1_grad, 64, 1)
    b1_grad = b1_grad + pltpu.roll(b1_grad, 32, 1)
    b2_grad = b2_grad + pltpu.roll(b2_grad, 64, 1)
    grad_ref[7, 0:32, :] = w1_grad * scale_first
    grad_ref[7, 32:40, :] = b1_grad * scale_first
    grad_ref[7, 40:48, :] = b2_grad * scale_second
    grad_ref[7, 48:64, :] = jnp.zeros((16, 128), F32)


def unpack_kernel(total_ref, w1_ref, b1_ref, w2_ref, b2_ref):
    for j in range(6):
        w2_ref[:, j * 128 : (j + 1) * 128] = total_ref[j].astype(F32)
    w2_ref[:, 768:864] = total_ref[6].astype(F32)[:, :96]
    rest = total_ref[7].astype(F32)
    w1_ref[...] = rest[0:32, 0:108]
    b1_ref[...] = rest[32:33, 0:32]
    b2_ref[...] = rest[40:41, 0:64]


def exchange(x, axes, count):
    sent = jnp.broadcast_to(x[None], (count,) + x.shape)
    return lax.all_to_all(sent, axes, 0, 0, tiled=True)


def sum_everywhere(packed):
    part = lax.all_to_all(packed, ("x", "c"), 0, 0, tiled=True)
    part = jnp.sum(part.astype(F32), axis=0)
    part = jnp.sum(exchange(part, ("yh", "yl"), 8), axis=0)
    part = jnp.sum(exchange(part, "z", 8), axis=0)
    return exchange(part, ("x", "c"), 8)


def local_step(volume, w1, b1, w2, b2, cotangent, space, count, cells):
    vol, cot = volume[0], cotangent[0]
    forward = [(i, i + 1) for i in range(count - 1)]
    backward = [(i + 1, i) for i in range(count - 1)]
    planes = vol.shape[1]
    edge = lambda plane: cot[:, plane].transpose(1, 0, 2).reshape(256, 128)
    vlo = lax.ppermute(vol[:, planes - HALO :], space, forward)
    vhi = lax.ppermute(vol[:, :HALO], space, backward)
    clo = lax.ppermute(edge(cot.shape[1] - 1), space, forward)
    chi = lax.ppermute(edge(0), space, backward)
    cot = cot.transpose(1, 2, 0, 3).reshape(4, 256, 128)
    w1big, wexp, wt = pl.pallas_call(
        prepare_kernel,
        out_shape=(
            jax.ShapeDtypeStruct((256, 256), BF16),
            jax.ShapeDtypeStruct((256, 1536), BF16),
            jax.ShapeDtypeStruct((384, 768), BF16),
        ),
        scratch_shapes=[pltpu.VMEM((64, 1024), F32)],
        compiler_params=pltpu.CompilerParams(vmem_limit_bytes=16 * 2**20),
        cost_estimate=pl.CostEstimate(flops=20_000_000, bytes_accessed=2_000_000, transcendentals=0),
        name="prepare",
    )(w1, w2, jnp.asarray(spread_matrix(), BF16))
    place = jnp.stack([lax.axis_index(space), jnp.int32(count - 1)]).astype(jnp.int32)
    b1x = jnp.broadcast_to(jnp.tile(b1, 8)[:, None], (256, 128))
    b2x = jnp.broadcast_to(jnp.tile(b2, 4)[:, None], (256, 128))

    def kernel(*refs):
        main_kernel(*refs, scale_first=1.0 / math.sqrt(cells), scale_second=1.0 / math.sqrt(cells / 8.0))

    vmem = pl.BlockSpec(memory_space=pltpu.VMEM)
    act, packed = pl.pallas_call(
        kernel,
        out_shape=(
            jax.ShapeDtypeStruct((4, 256, 128), BF16),
            jax.ShapeDtypeStruct((8, 64, 128), F32),
        ),
        in_specs=[pl.BlockSpec(memory_space=pltpu.SMEM)] + [vmem] * 13,
        out_specs=(vmem, vmem),
        scratch_shapes=[
            pltpu.VMEM((18 * 128, 128), F32),
            pltpu.VMEM((18, 160, 128), BF16),
            pltpu.VMEM((8 * 512, 128), BF16),
            pltpu.VMEM((6 * 256, 128), BF16),
            pltpu.VMEM((16, 256, 128), BF16),
        ],
        compiler_params=pltpu.CompilerParams(vmem_limit_bytes=48 * 2**20),
        cost_estimate=pl.CostEstimate(flops=3_000_000_000, bytes_accessed=4_000_000, transcendentals=0),
        name="layers",
    )(
        place, vol, vlo, vhi, cot, clo, chi,
        jnp.asarray(split_matrix(), BF16), jnp.asarray(compact_matrix(), F32),
        w1big, b1x, wexp, b2x, wt,
    )
    act = act.reshape(4, 4, 64, 128).transpose(2, 0, 1, 3)[None]
    return act, packed


def solution(mesh):
    dp, space = mesh.shape["dp"], mesh.shape["space"]
    split = Mesh(mesh.devices.reshape(8, 2, 4, 4, 2), ("z", "yh", "x", "yl", "c"))
    along = ("x", "yl", "c")

    def on_device(volume, w1, b1, w2, b2, cotangent):
        cells = float(math.prod(volume.shape[2:]) * dp * space)
        act, packed = local_step(volume, w1, b1, w2, b2, cotangent, along, space, cells)
        total = sum_everywhere(packed)
        gw1, gb1, gw2, gb2 = pl.pallas_call(
            unpack_kernel,
            out_shape=(
                jax.ShapeDtypeStruct((32, 108), F32),
                jax.ShapeDtypeStruct((1, 32), F32),
                jax.ShapeDtypeStruct((64, 864), F32),
                jax.ShapeDtypeStruct((1, 64), F32),
            ),
            name="unpack",
        )(total)
        return act, gw1, gb1[0], gw2, gb2[0]

    shared = P(("z", "yh"), None, along, None, None)
    return jax.shard_map(
        on_device,
        mesh=split,
        in_specs=(shared, P(), P(), P(), P(), shared),
        out_specs=(shared, P(), P(), P(), P()),
        check_vma=False,
    )
```

time: 364 us -> 91.5 us (0.25)
  waiting for transfers between devices: 103 us -> 5.63 us
  local copies, waits for them, and re-layouts: 84 us -> 5.25 us
  blocking collectives: 110 us -> 48.9 us
  other arithmetic: 16.8 us -> 0.13 us
  matrix products: 15.5 us -> 0 us
  between operations: 14.6 us -> 0.86 us
  Pallas kernels: 0 us -> 6.9 us
    psum x1 -> x0, blocking collectives: 110 us -> none  [on_device(): lax.psum((grad_first_weight, grad_first_bias, grad_second_weight, grad_se...]
    psum x1 -> x0, waiting for transfers between devices: 100 us -> none  [on_device(): lax.psum((grad_first_weight, grad_first_bias, grad_second_weight, grad_se...]
    all_to_all x0 -> x3, blocking collectives: none -> 48.9 us  [the longest x2 36 us: exchange(): return lax.all_to_all(sent, axes, 0, 0, tiled=True)]
    unnamed x95 -> x20, local copies, waits for them, and re-layouts: 30.6 us -> 2.21 us
    reshape x5 -> x1, local copies, waits for them, and re-layouts: 24.2 us -> 0.91 us  [local_step(): act = act.reshape(4, 4, 64, 128).transpose(2, 0, 1, 3)[None]]
    dot_general x5 -> x0, matrix products: 15.5 us -> none  [the longest x1 4.38 us: on_device(): jnp.dot(flipped, stacked_back, preferred_element_type=jnp.float32)]
    reduce_sum x2 -> x3, other arithmetic: 11.1 us -> 0.06 us  [the longest x1 0.02 us: sum_everywhere(): part = jnp.sum(part.astype(F32), axis=0)]
    all_to_all x0 -> x1, starting transfers between devices: none -> 7.4 us  [exchange(): return lax.all_to_all(sent, axes, 0, 0, tiled=True)]
  transfers between devices with their start and end apart: 7 -> 5, of which waited for: 2 -> 1; matrix products, arithmetic and copies ran while one was open for 20% -> 1% of each run, Pallas kernels for 0% -> 0%
where the time goes in v1:
time: 91.5 us; the launch traced here: 90.9 us
  blocking collectives  48.9 us (53%)
  starting transfers between devices  23.3 us (25%)
  Pallas kernels  6.9 us (8%)
  waiting for transfers between devices  5.63 us (6%)
  local copies, waits for them, and re-layouts  5.25 us (6%)
    all_to_all x2, blocking collectives, exchange(): return lax.all_to_all(sent, axes, 0, 0, tiled=True)  36 us
    all_to_all x1, blocking collectives, sum_everywhere(): part = lax.all_to_all(packed, ('x', 'c'), 0, 0, tiled=True)  12.9 us
    all_to_all x1, starting transfers between devices, exchange(): return lax.all_to_all(sent, axes, 0, 0, tiled=True)  7.4 us
    ppermute x1, starting transfers between devices, local_step(): chi = lax.ppermute(edge(0), space, backward)  5.62 us
    all_to_all x1, waiting for transfers between devices, exchange(): return lax.all_to_all(sent, axes, 0, 0, tiled=True)  5.62 us
    pallas_call x1, Pallas kernels, local_step(): pl.pallas_call(kernel, out_shape=(jax.ShapeDtypeStruct((4, 256, 128), BF1...  4.92 us
    ppermute x1, starting transfers between devices, local_step(): clo = lax.ppermute(edge(cot.shape[1] - 1), space, forward)  4.73 us
    ppermute x1, starting transfers between devices, local_step(): vlo = lax.ppermute(vol[:, planes - HALO:], space, forward)  3.64 us
  transfers between devices with their start and end apart: 5, of which 1 were waited for; matrix products, arithmetic and copies ran while one was open for 1% of the time, Pallas kernels for 0%

profile of v1, /device:TPU:1, one launch (start us, length us, event | category | flops | bytes accessed | tf_op | source)
XLA Modules:
  0.0 90.9 jit_solution(10567545712902206463)
XLA Ops:
  0.6 0.9 %slice_bitcast_fusion = (bf16[4,64,128]{2,0,1:T(4,128)(2,1)S(1)}, bf16[4,64,128]{2,0,1:T(4,128)(2,1)S(1)}) fusion(bf16[64,4,4,128]{3,2,1,0:T(4,128)(2,1)} %bitcast.28), kind=kLoop, calls=%fused_computation.1 | loop fusion | bytes 262144 | tf_op jit(solution)/shard_map/transpose | solution.py:267
  1.6 0.0 copy-start.1
  1.6 0.0 copy-start.7
  1.6 4.7 %collective-permute-start.2 = (bf16[256,128]{1,0:T(8,128)(2,1)S(1)}, bf16[256,128]{1,0:T(8,128)(2,1)S(1)}, u32[]{:S(2)}, u32[]{:S(2)}) collective-permute-start(bf16[256,128]{1,0:T(8,128)(2,1)S(1)} %bitcast.31), channel_id=1, source_target_pairs={{0,1},{1,2},{2,3},{3,4},{4,5},{5,6},{6,7},{7,8},{8,9},{9,10},{10,1... | collective-permute-start | bytes 196616 | tf_op jit(solution)/shard_map/ppermute | solution.py:270
  6.3 0.0 copy-start.8
  6.3 0.0 copy-start.9
  6.4 0.0 copy-start
  6.4 5.6 %collective-permute-start.3 = (bf16[256,128]{1,0:T(8,128)(2,1)S(1)}, bf16[256,128]{1,0:T(8,128)(2,1)S(1)}, u32[]{:S(2)}, u32[]{:S(2)}) collective-permute-start(bf16[256,128]{1,0:T(8,128)(2,1)S(1)} %bitcast.32), channel_id=1, source_target_pairs={{1,0},{2,1},{3,2},{4,3},{5,4},{6,5},{7,6},{8,7},{9,8},{10,9},{11,1... | collective-permute-start | bytes 196616 | tf_op jit(solution)/shard_map/ppermute | solution.py:271
  12.0 0.0 copy-done.1
  12.0 1.9 %collective-permute-start.1 = (bf16[4,5,8,256]{3,2,1,0:T(8,128)(2,1)S(1)}, bf16[4,5,8,256]{3,2,1,0:T(8,128)(2,1)S(1)}, u32[]{:S(2)}, u32[]{:S(2)}) collective-permute-start(bf16[4,5,8,256]{3,2,1,0:T(8,128)(2,1)S(1)} %get-tuple-element.25), channel_id=1, source_target_pairs={{1,0},{2,1},{3,2},{4,3},{5,4},{6,5},{7,6},{8,7},{9,8},{10,9},{11,1... | collective-permute-start | bytes 245768 | tf_op jit(solution)/shard_map/ppermute | solution.py:269
  14.0 3.6 %collective-permute-start = (bf16[4,5,8,256]{3,2,1,0:T(8,128)(2,1)S(1)}, bf16[4,5,8,256]{3,2,1,0:T(8,128)(2,1)S(1)}, u32[]{:S(2)}, u32[]{:S(2)}) collective-permute-start(bf16[4,5,8,256]{3,2,1,0:T(8,128)(2,1)S(1)} %get-tuple-element.26), channel_id=1, source_target_pairs={{0,1},{1,2},{2,3},{3,4},{4,5},{5,6},{6,7},{7,8},{8,9},{9,10},{10,1... | collective-permute-start | bytes 245768 | tf_op jit(solution)/shard_map/ppermute | solution.py:268
  17.6 0.0 copy-done.8
  17.6 0.1 broadcast_in_dim.18
  17.7 0.0 copy-done.9
  17.7 0.1 broadcast_in_dim.16
  17.8 0.0 copy-done.7
  17.8 0.0 copy-start.2
  17.8 0.0 copy-start.3
  17.8 0.1 copy.18
  17.9 0.0 copy-done
  17.9 0.8 copy-done.2
  18.7 0.0 copy-done.3
  18.7 0.0 copy-start.5
  18.7 0.3 prepare.1
  19.1 0.0 copy-start.4
  19.1 0.1 pad_add_fusion.refs_0_
  19.1 0.0 collective-permute-done.2.refs_5_
  19.1 0.0 collective-permute-done.3.refs_6_
  19.1 0.0 collective-permute-done.1.refs_3_
  19.2 0.0 collective-permute-done.refs_2_
  19.2 0.1 broadcast_in_dim.17.refs_10_
  19.3 0.1 broadcast_in_dim.38.refs_12_
  19.4 0.3 copy-done.5
  19.6 0.4 copy-done.4
  20.0 4.9 %layers.1 = (bf16[4,256,128]{2,1,0:T(8,128)(2,1)S(1)}, f32[8,64,128]{2,1,0:T(8,128)S(1)}) custom-call(s32[2]{0:T(128)S(1)} %pad_add_fusion.refs_0_, bf16[4,8,8,256]{3,2,1,0:T(8,128)(2,1)S(1)} %bitcast.27, bf16[4,5,8,256]{3,2,1,0:T(8,128)(2,1)S(1)} %collective-permute-done.refs_2_, bf16[4,5,8,256]{3,2,1,0:T(8,128)(2,1)S(1)} %collective-permute-done.1.refs_3_, ...), custom_call_target="tpu_custom_call" | custom-call | flops 3000000000 | bytes 4000000 | tf_op jit(solution)/shard_map/layers/pallas_call | solution.py:293
  24.9 12.9 %all_to_all.20 = f32[8,64,128]{2,1,0:T(8,128)S(1)} all-to-all(f32[8,64,128]{2,1,0:T(8,128)S(1)} %get-tuple-element.18), channel_id=1, replica_groups=mesh['z'=8,'yh'=2,'x'=4,'yl'=4,'c'=2] {'x','c'}, dimensions={0} | all-to-all | bytes 524288 | tf_op jit(solution)/shard_map/all_to_all | solution.py:255
  37.9 16.7 %all_to_all.21 = f32[8,64,128]{2,1,0:T(8,128)S(1)} all-to-all(f32[8,64,128]{2,1,0:T(8,128)S(1)} %broadcast_in_dim.40), channel_id=1, replica_groups=mesh['z'=8,'yh'=2,'x'=4,'yl'=4,'c'=2] {'yh','yl'}, dimensions={0} | all-to-all | bytes 524288 | tf_op jit(solution)/shard_map/all_to_all | solution.py:251
  54.7 19.3 %all_to_all.22 = f32[8,64,128]{2,1,0:T(8,128)S(1)} all-to-all(f32[8,64,128]{2,1,0:T(8,128)S(1)} %broadcast_in_dim.41), channel_id=1, replica_groups=mesh['z'=8,'yh'=2,'x'=4,'yl'=4,'c'=2] {'z'}, dimensions={0} | all-to-all | bytes 524288 | tf_op jit(solution)/shard_map/all_to_all | solution.py:251
  73.9 0.7 broadcast_in_dim.42
  74.7 7.4 %all-to-all-start.3 = ((f32[8,64,128]{2,1,0:T(8,128)}), f32[8,64,128]{2,1,0:T(8,128)S(1)}, u32[]{:S(2)}, u32[]{:S(2)}) async-start(f32[8,64,128]{2,1,0:T(8,128)} %broadcast_in_dim.42), calls=%async_computation.3 | async-start | bytes 524288 | tf_op jit(solution)/shard_map/all_to_all | solution.py:251
  82.1 0.9 copy.23
  83.0 5.6 %all-to-all-done.3.total_ref = f32[8,64,128]{2,1,0:T(8,128)S(1)} async-done(((f32[8,64,128]{2,1,0:T(8,128)}), f32[8,64,128]{2,1,0:T(8,128)S(1)}, u32[]{:S(2)}, u32[]{:S(2)}) %all-to-all-start.3) | async-done | bytes 262176 | tf_op jit(solution)/shard_map/all_to_all | solution.py:251
  88.6 0.0 copy-start.6
  88.6 0.7 copy-done.6
  89.3 1.7 %unpack.1 = (f32[32,108]{1,0:T(8,128)}, f32[1,32]{1,0:T(1,128)}, f32[64,864]{1,0:T(8,128)}, f32[1,64]{1,0:T(1,128)}) custom-call(f32[8,64,128]{2,1,0:T(8,128)} %copy-done.6), custom_call_target="tpu_custom_call" | custom-call | tf_op jit(solution)/shard_map/unpack/pallas_call | solution.py:329
  (10 shorter events, 0.1 us)
Async XLA Ops:
  1.6 10.5 %copy-start.1 = (bf16[1,4,8,8,256]{4,3,2,1,0:T(8,128)(2,1)S(1)}, bf16[1,4,8,8,256]{4,3,2,1,0:T(8,128)(2,1)}, u32[]{:S(2)}) copy-start(bf16[1,4,8,8,256]{4,3,2,1,0:T(8,128)(2,1)} %param.9) | copy-start | bytes 393220
  1.6 16.2 %copy-start.7 = (bf16[1,64,4,4,128]{4,3,2,1,0:T(4,128)(2,1)S(1)}, bf16[1,64,4,4,128]{4,3,2,1,0:T(4,128)(2,1)}, u32[]{:S(2)}) copy-start(bf16[1,64,4,4,128]{4,3,2,1,0:T(4,128)(2,1)} %param.14) | copy-start | bytes 786436
  1.6 17.5 %collective-permute-start.2 = (bf16[256,128]{1,0:T(8,128)(2,1)S(1)}, bf16[256,128]{1,0:T(8,128)(2,1)S(1)}, u32[]{:S(2)}, u32[]{:S(2)}) collective-permute-start(bf16[256,128]{1,0:T(8,128)(2,1)S(1)} %bitcast.31), channel_id=1, source_target_pairs={{0,1},{1,2},{2,3},{3,4},{4,5},{5,6},{6,7},{7,8},{8,9},{9,10},{10,1... | collective-permute-start | bytes 196616 | tf_op jit(solution)/shard_map/ppermute | solution.py:270
  6.3 11.3 %copy-start.8 = (f32[64]{0:T(128)S(1)}, f32[64]{0:T(128)}, u32[]{:S(2)}) copy-start(f32[64]{0:T(128)} %param.13) | copy-start | bytes 772
  6.3 11.4 %copy-start.9 = (f32[32]{0:T(128)S(1)}, f32[32]{0:T(128)}, u32[]{:S(2)}) copy-start(f32[32]{0:T(128)} %param.11) | copy-start | bytes 388
  6.4 11.5 %copy-start = (bf16[108,2048]{1,0:T(8,128)(2,1)S(1)}, bf16[108,2048]{1,0:T(8,128)(2,1)}, u32[]{:S(2)}) copy-start(bf16[108,2048]{1,0:T(8,128)(2,1)} %constant.25.clone.sel_ref) | copy-start | bytes 1327108
  6.4 12.8 %collective-permute-start.3 = (bf16[256,128]{1,0:T(8,128)(2,1)S(1)}, bf16[256,128]{1,0:T(8,128)(2,1)S(1)}, u32[]{:S(2)}, u32[]{:S(2)}) collective-permute-start(bf16[256,128]{1,0:T(8,128)(2,1)S(1)} %bitcast.32), channel_id=1, source_target_pairs={{1,0},{2,1},{3,2},{4,3},{5,4},{6,5},{7,6},{8,7},{9,8},{10,9},{11,1... | collective-permute-start | bytes 196616 | tf_op jit(solution)/shard_map/ppermute | solution.py:271
  12.0 7.1 %collective-permute-start.1 = (bf16[4,5,8,256]{3,2,1,0:T(8,128)(2,1)S(1)}, bf16[4,5,8,256]{3,2,1,0:T(8,128)(2,1)S(1)}, u32[]{:S(2)}, u32[]{:S(2)}) collective-permute-start(bf16[4,5,8,256]{3,2,1,0:T(8,128)(2,1)S(1)} %get-tuple-element.25), channel_id=1, source_target_pairs={{1,0},{2,1},{3,2},{4,3},{5,4},{6,5},{7,6},{8,7},{9,8},{10,9},{11,1... | collective-permute-start | bytes 245768 | tf_op jit(solution)/shard_map/ppermute | solution.py:269
  14.0 5.2 %collective-permute-start = (bf16[4,5,8,256]{3,2,1,0:T(8,128)(2,1)S(1)}, bf16[4,5,8,256]{3,2,1,0:T(8,128)(2,1)S(1)}, u32[]{:S(2)}, u32[]{:S(2)}) collective-permute-start(bf16[4,5,8,256]{3,2,1,0:T(8,128)(2,1)S(1)} %get-tuple-element.26), channel_id=1, source_target_pairs={{0,1},{1,2},{2,3},{3,4},{4,5},{5,6},{6,7},{7,8},{8,9},{9,10},{10,1... | collective-permute-start | bytes 245768 | tf_op jit(solution)/shard_map/ppermute | solution.py:268
  17.8 0.9 copy-start.2
  17.8 0.9 copy-start.3
  18.7 0.9 copy-start.5
  19.1 1.0 %copy-start.4 = (bf16[256,512]{1,0:T(8,128)(2,1)S(1)}, bf16[256,512]{1,0:T(8,128)(2,1)}, u32[]{:S(2)}) copy-start(bf16[256,512]{1,0:T(8,128)(2,1)} %constant.26.clone.refs_7_) | copy-start | bytes 786436
  74.7 13.9 %all-to-all-start.3 = ((f32[8,64,128]{2,1,0:T(8,128)}), f32[8,64,128]{2,1,0:T(8,128)S(1)}, u32[]{:S(2)}, u32[]{:S(2)}) async-start(f32[8,64,128]{2,1,0:T(8,128)} %broadcast_in_dim.42), calls=%async_computation.3 | async-start | bytes 524288 | tf_op jit(solution)/shard_map/all_to_all | solution.py:251
  88.6 0.7 copy-start.6

commit v2 on v1

--- a/solution.py
+++ b/solution.py
@@ -74,7 +74,7 @@
 
 
 def main_kernel(
-    place_ref, vol_ref, vlo_ref, vhi_ref, cot_ref, clo_ref, chi_ref, split_ref, compact_ref,
+    place_ref, vol_ref, low_ref, high_ref, cot_ref, split_ref, compact_ref,
     w1_ref, b1_ref, wexp_ref, b2_ref, wt_ref,
     act_ref, grad_ref,
     fine, win, ps, g2s, pre_s,
@@ -83,8 +83,11 @@
     place = place_ref[0]
     last = place_ref[1]
     x0 = 0
-    for ref, count in ((vlo_ref, HALO), (vol_ref, 8), (vhi_ref, HALO)):
-        rows = ref[...].astype(F32).reshape(4 * count * 8, 256).astype(BF16)
+    for ref, count in ((low_ref, HALO), (vol_ref, 8), (high_ref, HALO)):
+        if ref is vol_ref:
+            rows = ref[...].astype(F32).reshape(4 * count * 8, 256).astype(BF16)
+        else:
+            rows = ref[0 : 4 * count * 8, :]
         parts = jnp.dot(rows, split_ref[...], preferred_element_type=F32)
         for c in range(4):
             for x in range(count):
@@ -139,7 +142,13 @@
         act = jnp.maximum(pre, leak_slope * pre)
         for i in range(2):
             r = r0 + i
-            cot = (clo_ref[...] if r == 0 else chi_ref[...] if r == 5 else cot_ref[r - 1]).astype(F32)
+            if 1 <= r <= 4:
+                cot = cot_ref[r - 1].astype(F32)
+            else:
+                sent = (low_ref if r == 0 else high_ref)[160:288, :].astype(F32)
+                cot = jnp.concatenate(
+                    [sent[0:64, 0:128], sent[64:128, 0:128], sent[0:64, 128:256], sent[64:128, 128:256]], axis=0
+                )
             own = pre[:, i * 128 : (i + 1) * 128]
             g2s[r * 256 : (r + 1) * 256, :] = jnp.where(own > 0, cot, leak_slope * cot).astype(BF16)
             if 1 <= r <= 4:
@@ -170,9 +179,9 @@
     lane128 = lax.broadcasted_iota(jnp.int32, (128, 128), 1)
     for j in range(0, 8, 2):
         two = jnp.where(lane128 < 64, folded[j * 128 : (j + 1) * 128], folded[(j + 1) * 128 : (j + 2) * 128]).T
-        grad_ref[j] = two[:64]
+        grad_ref[j] = two[:64].astype(BF16)
         if j < 6:
-            grad_ref[j + 1] = two[64:]
+            grad_ref[j + 1] = two[64:].astype(BF16)
 
     ones16 = jnp.ones((16, 512), BF16)
     m1 = None
@@ -230,10 +239,10 @@
     b1_grad = b1_grad + pltpu.roll(b1_grad, 64, 1)
     b1_grad = b1_grad + pltpu.roll(b1_grad, 32, 1)
     b2_grad = b2_grad + pltpu.roll(b2_grad, 64, 1)
-    grad_ref[7, 0:32, :] = w1_grad * scale_first
-    grad_ref[7, 32:40, :] = b1_grad * scale_first
-    grad_ref[7, 40:48, :] = b2_grad * scale_second
-    grad_ref[7, 48:64, :] = jnp.zeros((16, 128), F32)
+    biases = jnp.concatenate([b1_grad * scale_first, b2_grad * scale_second], axis=0)
+    grad_ref[7, 0:32, :] = (w1_grad * scale_first).astype(BF16)
+    grad_ref[7, 32:48, :] = biases.astype(BF16)
+    grad_ref[7, 48:64, :] = jnp.zeros((16, 128), BF16)
 
 
 def unpack_kernel(total_ref, w1_ref, b1_ref, w2_ref, b2_ref):
@@ -247,15 +256,18 @@
 
 
 def exchange(x, axes, count):
-    sent = jnp.broadcast_to(x[None], (count,) + x.shape)
+    sent = jnp.broadcast_to(x.astype(BF16)[None], (count,) + x.shape)
     return lax.all_to_all(sent, axes, 0, 0, tiled=True)
 
 
+def add(parts):
+    return jnp.sum(parts.astype(F32), axis=0)
+
+
 def sum_everywhere(packed):
-    part = lax.all_to_all(packed, ("x", "c"), 0, 0, tiled=True)
-    part = jnp.sum(part.astype(F32), axis=0)
-    part = jnp.sum(exchange(part, ("yh", "yl"), 8), axis=0)
-    part = jnp.sum(exchange(part, "z", 8), axis=0)
+    part = add(lax.all_to_all(packed, ("x", "c"), 0, 0, tiled=True))
+    part = add(exchange(part, ("yh", "yl"), 8))
+    part = add(exchange(part, "z", 8))
     return exchange(part, ("x", "c"), 8)
 
 
@@ -264,11 +276,14 @@
     forward = [(i, i + 1) for i in range(count - 1)]
     backward = [(i + 1, i) for i in range(count - 1)]
     planes = vol.shape[1]
-    edge = lambda plane: cot[:, plane].transpose(1, 0, 2).reshape(256, 128)
-    vlo = lax.ppermute(vol[:, planes - HALO :], space, forward)
-    vhi = lax.ppermute(vol[:, :HALO], space, backward)
-    clo = lax.ppermute(edge(cot.shape[1] - 1), space, forward)
-    chi = lax.ppermute(edge(0), space, backward)
+
+    def edge(first, plane):
+        planes_sent = vol[:, first : first + HALO].reshape(160, 256)
+        rows = cot[:, plane].reshape(64, 2, 2, 128).transpose(2, 0, 1, 3).reshape(128, 256)
+        return jnp.concatenate([planes_sent, rows], axis=0)
+
+    low = lax.ppermute(edge(planes - HALO, cot.shape[1] - 1), space, forward)
+    high = lax.ppermute(edge(0, 0), space, backward)
     cot = cot.transpose(1, 2, 0, 3).reshape(4, 256, 128)
     w1big, wexp, wt = pl.pallas_call(
         prepare_kernel,
@@ -294,9 +309,9 @@
         kernel,
         out_shape=(
             jax.ShapeDtypeStruct((4, 256, 128), BF16),
-            jax.ShapeDtypeStruct((8, 64, 128), F32),
+            jax.ShapeDtypeStruct((8, 64, 128), BF16),
         ),
-        in_specs=[pl.BlockSpec(memory_space=pltpu.SMEM)] + [vmem] * 13,
+        in_specs=[pl.BlockSpec(memory_space=pltpu.SMEM)] + [vmem] * 11,
         out_specs=(vmem, vmem),
         scratch_shapes=[
             pltpu.VMEM((18 * 128, 128), F32),
@@ -309,7 +324,7 @@
         cost_estimate=pl.CostEstimate(flops=3_000_000_000, bytes_accessed=4_000_000, transcendentals=0),
         name="layers",
     )(
-        place, vol, vlo, vhi, cot, clo, chi,
+        place, vol, low, high, cot,
         jnp.asarray(split_matrix(), BF16), jnp.asarray(compact_matrix(), F32),
         w1big, b1x, wexp, b2x, wt,
     )

time: 91.5 us -> 78.9 us (0.86)
  blocking collectives: 48.9 us -> 42.8 us
  starting transfers between devices: 23.3 us -> 17.3 us
  waiting for transfers between devices: 5.63 us -> 4.39 us
    ppermute x4 -> x2, starting transfers between devices: 15.9 us -> 10.2 us  [the longest x1 5.62 us: local_step(): high = lax.ppermute(edge(0, 0), space, backward)]
    all_to_all x1, blocking collectives: 12.9 us -> 9.51 us  [sum_everywhere(): part = add(lax.all_to_all(packed, ('x', 'c'), 0, 0, tiled=True))]
    all_to_all x2, blocking collectives: 36 us -> 33.3 us  [exchange(): return lax.all_to_all(sent, axes, 0, 0, tiled=True)]
    all_to_all x1, waiting for transfers between devices: 5.62 us -> 4.39 us  [exchange(): return lax.all_to_all(sent, axes, 0, 0, tiled=True)]
    transpose x3 -> x0, local copies, waits for them, and re-layouts: 0.94 us -> none  [local_step(): edge = lambda plane: cot[:, plane].transpose(1, 0, 2).reshape(256, 128)]
    slice x1 -> x2, local copies, waits for them, and re-layouts: 0.01 us -> 0.93 us  [the longest x1 0.92 us: edge(): cot[:, plane].reshape(64, 2, 2, 128).transpose(2, 0, 1, 3).reshape(128, 256)]
    unnamed x20 -> x22, local copies, waits for them, and re-layouts: 2.21 us -> 3.01 us
  transfers between devices with their start and end apart: 5 -> 3, of which waited for: 1 -> 1; matrix products, arithmetic and copies ran while one was open for 1% -> 2% of each run, Pallas kernels for 0% -> 0%
where the time goes in v2:
time: 78.9 us; the launch traced here: 78.4 us
  blocking collectives  42.8 us (54%)
  starting transfers between devices  17.3 us (22%)
  Pallas kernels  6.83 us (9%)
  local copies, waits for them, and re-layouts  6.05 us (8%)
  waiting for transfers between devices  4.39 us (6%)
  between operations  0.85 us (1%)
    all_to_all x2, blocking collectives, exchange(): return lax.all_to_all(sent, axes, 0, 0, tiled=True)  33.3 us
    all_to_all x1, blocking collectives, sum_everywhere(): part = add(lax.all_to_all(packed, ('x', 'c'), 0, 0, tiled=True))  9.51 us
    all_to_all x1, starting transfers between devices, exchange(): return lax.all_to_all(sent, axes, 0, 0, tiled=True)  7.07 us
    ppermute x1, starting transfers between devices, local_step(): high = lax.ppermute(edge(0, 0), space, backward)  5.62 us
    pallas_call x1, Pallas kernels, local_step(): pl.pallas_call(kernel, out_shape=(jax.ShapeDtypeStruct((4, 256, 128), BF1...  4.89 us
    ppermute x1, starting transfers between devices, local_step(): low = lax.ppermute(edge(planes - HALO, cot.shape[1] - 1), space, forward)  4.59 us
    all_to_all x1, waiting for transfers between devices, exchange(): return lax.all_to_all(sent, axes, 0, 0, tiled=True)  4.39 us
    unnamed x22, local copies, waits for them, and re-layouts  3.01 us
  transfers between devices with their start and end apart: 3, of which 1 were waited for; matrix products, arithmetic and copies ran while one was open for 2% of the time, Pallas kernels for 0%

profile of v2, /device:TPU:1, one launch (start us, length us, event | category | flops | bytes accessed | tf_op | source)
XLA Modules:
  0.0 78.4 jit_solution(9477516953276216476)
XLA Ops:
  0.6 0.9 %fusion = (bf16[64,1,4,128]{3,2,1,0:T(4,128)(2,1)S(1)}, bf16[64,1,4,128]{3,2,1,0:T(4,128)(2,1)S(1)}) fusion(bf16[64,4,4,128]{3,2,1,0:T(4,128)(2,1)} %bitcast.34), kind=kLoop, calls=%fused_computation.6 | loop fusion | bytes 262144 | tf_op jit(solution)/shard_map/slice | solution.py:282
  1.6 0.0 copy-start.1
  1.6 0.8 %copy-done.1 = bf16[1,4,8,8,256]{4,3,2,1,0:T(8,128)(2,1)S(1)} copy-done((bf16[1,4,8,8,256]{4,3,2,1,0:T(8,128)(2,1)S(1)}, bf16[1,4,8,8,256]{4,3,2,1,0:T(8,128)(2,1)}, u32[]{:S(2)}) %copy-start.1) | copy-done | bytes 131096
  2.5 4.6 %collective-permute-start = (bf16[288,256]{1,0:T(8,128)(2,1)S(1)}, bf16[288,256]{1,0:T(8,128)(2,1)S(1)}, u32[]{:S(2)}, u32[]{:S(2)}) collective-permute-start(bf16[288,256]{1,0:T(8,128)(2,1)S(1)} %pad_maximum_fusion), channel_id=1, source_target_pairs={{0,1},{1,2},{2,3},{3,4},{4,5},{5,6},{6,7},{7,8},{8,9},{9,10},{10,1... | collective-permute-start | bytes 442376 | tf_op jit(solution)/shard_map/ppermute | solution.py:285
  7.1 0.0 copy-start.6
  7.2 0.0 copy-start.8
  7.2 0.0 copy-start.9
  7.2 0.0 copy-start
  7.2 5.6 %collective-permute-start.1 = (bf16[288,256]{1,0:T(8,128)(2,1)S(1)}, bf16[288,256]{1,0:T(8,128)(2,1)S(1)}, u32[]{:S(2)}, u32[]{:S(2)}) collective-permute-start(bf16[288,256]{1,0:T(8,128)(2,1)S(1)} %pad_maximum_fusion.1), channel_id=1, source_target_pairs={{1,0},{2,1},{3,2},{4,3},{5,4},{6,5},{7,6},{8,7},{9,8},{10,9},{11,1... | collective-permute-start | bytes 442376 | tf_op jit(solution)/shard_map/ppermute | solution.py:286
  12.9 0.0 copy-done.8
  12.9 0.1 broadcast_in_dim.18
  13.0 0.0 copy-done.9
  13.0 0.1 broadcast_in_dim.16
  13.1 0.0 copy-done.6
  13.1 0.0 copy-start.2
  13.1 0.0 copy-start.3
  13.1 0.1 copy.20
  13.2 0.0 copy-done
  13.2 0.8 %copy-done.2 = bf16[64,864]{1,0:T(8,128)(2,1)S(1)} copy-done((bf16[64,864]{1,0:T(8,128)(2,1)S(1)}, bf16[64,864]{1,0:T(8,128)(2,1)}, u32[]{:S(2)}) %copy-start.2) | copy-done | bytes 110616
  14.0 0.0 copy-done.3
  14.0 0.0 copy-start.5
  14.0 0.3 prepare.1
  14.3 0.0 copy-start.4
  14.3 0.1 pad_add_fusion.refs_0_
  14.4 0.0 collective-permute-done.refs_2_
  14.4 0.0 collective-permute-done.1.refs_3_
  14.4 0.1 broadcast_in_dim.17.refs_8_
  14.5 0.1 broadcast_in_dim.38.refs_10_
  14.6 0.3 copy-done.5
  14.9 0.4 copy-done.4
  15.3 4.9 %layers.1 = (bf16[4,256,128]{2,1,0:T(8,128)(2,1)S(1)}, bf16[8,64,128]{2,1,0:T(8,128)(2,1)S(1)}) custom-call(s32[2]{0:T(128)S(1)} %pad_add_fusion.refs_0_, bf16[4,8,8,256]{3,2,1,0:T(8,128)(2,1)S(1)} %bitcast.33, bf16[288,256]{1,0:T(8,128)(2,1)S(1)} %collective-permute-done.refs_2_, bf16[288,256]{1,0:T(8,128)(2,1)S(1)} %collective-permute-done.1.refs_3_, ...), custom_call_target="tpu_custom_call" | custom-call | flops 3000000000 | bytes 4000000 | tf_op jit(solution)/shard_map/layers/pallas_call | solution.py:308
  20.2 9.5 %all_to_all.20 = bf16[8,64,128]{2,1,0:T(8,128)(2,1)S(1)} all-to-all(bf16[8,64,128]{2,1,0:T(8,128)(2,1)S(1)} %get-tuple-element.18), channel_id=1, replica_groups=mesh['z'=8,'yh'=2,'x'=4,'yl'=4,'c'=2] {'x','c'}, dimensions={0} | all-to-all | bytes 262144 | tf_op jit(solution)/shard_map/all_to_all | solution.py:268
  29.7 15.5 %all_to_all.21 = bf16[8,64,128]{2,1,0:T(8,128)(2,1)S(1)} all-to-all(bf16[8,64,128]{2,1,0:T(8,128)(2,1)S(1)} %broadcast_in_dim.40), channel_id=1, replica_groups=mesh['z'=8,'yh'=2,'x'=4,'yl'=4,'c'=2] {'yh','yl'}, dimensions={0} | all-to-all | bytes 262144 | tf_op jit(solution)/shard_map/all_to_all | solution.py:260
  45.3 17.8 %all_to_all.22 = bf16[8,64,128]{2,1,0:T(8,128)(2,1)S(1)} all-to-all(bf16[8,64,128]{2,1,0:T(8,128)(2,1)S(1)} %broadcast_in_dim.41), channel_id=1, replica_groups=mesh['z'=8,'yh'=2,'x'=4,'yl'=4,'c'=2] {'z'}, dimensions={0} | all-to-all | bytes 262144 | tf_op jit(solution)/shard_map/all_to_all | solution.py:260
  63.1 0.7 broadcast_in_dim.42
  63.8 7.1 %all-to-all-start.3 = ((bf16[8,64,128]{2,1,0:T(8,128)(2,1)}), bf16[8,64,128]{2,1,0:T(8,128)(2,1)S(1)}, u32[]{:S(2)}, u32[]{:S(2)}) async-start(bf16[8,64,128]{2,1,0:T(8,128)(2,1)} %broadcast_in_dim.42), calls=%async_computation.3 | async-start | bytes 262144 | tf_op jit(solution)/shard_map/all_to_all | solution.py:260
  70.9 0.9 %copy.27 = bf16[4,4,64,128]{3,1,0,2:T(4,128)(2,1)} copy(bf16[4,4,64,128]{3,2,1,0:T(8,128)(2,1)S(1)} %bitcast.31) | data formatting | bytes 524288 | tf_op jit(solution)/shard_map/reshape | solution.py:331
  71.8 4.4 %all-to-all-done.3.total_ref = bf16[8,64,128]{2,1,0:T(8,128)(2,1)S(1)} async-done(((bf16[8,64,128]{2,1,0:T(8,128)(2,1)}), bf16[8,64,128]{2,1,0:T(8,128)(2,1)S(1)}, u32[]{:S(2)}, u32[]{:S(2)}) %all-to-all-start.3) | async-done | bytes 131104 | tf_op jit(solution)/shard_map/all_to_all | solution.py:260
  76.1 0.0 copy-start.7
  76.2 0.6 copy-done.7
  76.8 1.6 %unpack.1 = (f32[32,108]{1,0:T(8,128)}, f32[1,32]{1,0:T(1,128)}, f32[64,864]{1,0:T(8,128)}, f32[1,64]{1,0:T(1,128)}) custom-call(bf16[8,64,128]{2,1,0:T(8,128)(2,1)} %copy-done.7), custom_call_target="tpu_custom_call" | custom-call | tf_op jit(solution)/shard_map/unpack/pallas_call | solution.py:344
  (14 shorter events, 0.2 us)
Async XLA Ops:
  1.6 0.9 %copy-start.1 = (bf16[1,4,8,8,256]{4,3,2,1,0:T(8,128)(2,1)S(1)}, bf16[1,4,8,8,256]{4,3,2,1,0:T(8,128)(2,1)}, u32[]{:S(2)}) copy-start(bf16[1,4,8,8,256]{4,3,2,1,0:T(8,128)(2,1)} %param.9) | copy-start | bytes 393220
  2.5 11.9 %collective-permute-start = (bf16[288,256]{1,0:T(8,128)(2,1)S(1)}, bf16[288,256]{1,0:T(8,128)(2,1)S(1)}, u32[]{:S(2)}, u32[]{:S(2)}) collective-permute-start(bf16[288,256]{1,0:T(8,128)(2,1)S(1)} %pad_maximum_fusion), channel_id=1, source_target_pairs={{0,1},{1,2},{2,3},{3,4},{4,5},{5,6},{6,7},{7,8},{8,9},{9,10},{10,1... | collective-permute-start | bytes 442376 | tf_op jit(solution)/shard_map/ppermute | solution.py:285
  7.1 5.9 %copy-start.6 = (bf16[1,64,4,4,128]{4,3,2,1,0:T(4,128)(2,1)S(1)}, bf16[1,64,4,4,128]{4,3,2,1,0:T(4,128)(2,1)}, u32[]{:S(2)}) copy-start(bf16[1,64,4,4,128]{4,3,2,1,0:T(4,128)(2,1)} %param.14) | copy-start | bytes 786436
  7.2 5.7 %copy-start.8 = (f32[64]{0:T(128)S(1)}, f32[64]{0:T(128)}, u32[]{:S(2)}) copy-start(f32[64]{0:T(128)} %param.13) | copy-start | bytes 772
  7.2 5.8 %copy-start.9 = (f32[32]{0:T(128)S(1)}, f32[32]{0:T(128)}, u32[]{:S(2)}) copy-start(f32[32]{0:T(128)} %param.11) | copy-start | bytes 388
  7.2 6.0 %copy-start = (bf16[108,2048]{1,0:T(8,128)(2,1)S(1)}, bf16[108,2048]{1,0:T(8,128)(2,1)}, u32[]{:S(2)}) copy-start(bf16[108,2048]{1,0:T(8,128)(2,1)} %constant.28.clone.sel_ref) | copy-start | bytes 1327108
  7.2 7.2 %collective-permute-start.1 = (bf16[288,256]{1,0:T(8,128)(2,1)S(1)}, bf16[288,256]{1,0:T(8,128)(2,1)S(1)}, u32[]{:S(2)}, u32[]{:S(2)}) collective-permute-start(bf16[288,256]{1,0:T(8,128)(2,1)S(1)} %pad_maximum_fusion.1), channel_id=1, source_target_pairs={{1,0},{2,1},{3,2},{4,3},{5,4},{6,5},{7,6},{8,7},{9,8},{10,9},{11,1... | collective-permute-start | bytes 442376 | tf_op jit(solution)/shard_map/ppermute | solution.py:286
  13.1 0.9 %copy-start.2 = (bf16[64,864]{1,0:T(8,128)(2,1)S(1)}, bf16[64,864]{1,0:T(8,128)(2,1)}, u32[]{:S(2)}) copy-start(bf16[64,864]{1,0:T(8,128)(2,1)} %w2_ref.1) | copy-start | bytes 331780
  13.1 0.9 %copy-start.3 = (bf16[32,108]{1,0:T(8,128)(2,1)S(1)}, bf16[32,108]{1,0:T(8,128)(2,1)}, u32[]{:S(2)}) copy-start(bf16[32,108]{1,0:T(8,128)(2,1)} %w1_ref.1) | copy-start | bytes 20740
  14.0 0.9 %copy-start.5 = (f32[256,128]{1,0:T(8,128)S(1)}, f32[256,128]{1,0:T(8,128)}, u32[]{:S(2)}) copy-start(f32[256,128]{1,0:T(8,128)} %constant.30.clone.refs_6_) | copy-start | bytes 393220
  14.3 1.0 %copy-start.4 = (bf16[256,512]{1,0:T(8,128)(2,1)S(1)}, bf16[256,512]{1,0:T(8,128)(2,1)}, u32[]{:S(2)}) copy-start(bf16[256,512]{1,0:T(8,128)(2,1)} %constant.29.clone.refs_5_) | copy-start | bytes 786436
  63.8 12.4 %all-to-all-start.3 = ((bf16[8,64,128]{2,1,0:T(8,128)(2,1)}), bf16[8,64,128]{2,1,0:T(8,128)(2,1)S(1)}, u32[]{:S(2)}, u32[]{:S(2)}) async-start(bf16[8,64,128]{2,1,0:T(8,128)(2,1)} %broadcast_in_dim.42), calls=%async_computation.3 | async-start | bytes 262144 | tf_op jit(solution)/shard_map/all_to_all | solution.py:260
  76.1 0.6 copy-start.7

commit v3 on v0

v3 whole, which is shorter than its diff:
```python
import math

import jax
import jax.numpy as jnp
import numpy as np
from jax import lax
from jax.experimental import pallas as pl
from jax.experimental.pallas import tpu as pltpu
from jax.sharding import Mesh, PartitionSpec as P

leak_slope = 0.3
F32, BF16 = jnp.float32, jnp.bfloat16
HALO = 5
NT = (((1,), (1,)), ((), ()))


def edges_kernel(space, vol_ref, cot_ref, pair_ref, other_ref, cot_s, sems):
    second = lax.axis_index(space) % 2
    copies = []
    for side, ref, high in ((0, other_ref, second), (1, pair_ref, 1 - second)):
        copies.append(pltpu.make_async_copy(cot_ref.at[:, high * 3], cot_s.at[side], sems.at[side, 4]))
        for c in range(4):
            source = vol_ref.at[c, pl.ds(high * (8 - HALO), HALO)]
            copies.append(pltpu.make_async_copy(source, ref.at[pl.ds(c * HALO, HALO)], sems.at[side, c]))
    for copy in copies:
        copy.start()
    for copy in copies:
        copy.wait()
    for side, ref in ((0, other_ref), (1, pair_ref)):
        rows = cot_s[side].astype(F32).reshape(256, 128)
        rows = jnp.concatenate([rows[:128], rows[128:]], axis=1)
        ref[4 * HALO : 4 * HALO + 16] = rows.astype(BF16).reshape(16, 8, 256)


def add_kernel(parts_ref, out_ref):
    total = jnp.sum(parts_ref[...].astype(F32), axis=0).astype(BF16)
    for i in range(out_ref.shape[0]):
        out_ref[i] = total


def in_hbm(x):
    return pltpu.with_memory_space_constraint(x, pltpu.HBM)


def cell_shift(s):
    return (s // 2 % 2) * 64 + (s % 2) * 16 + (s // 4) * 4


def split_phases(rows, split, count, fine, win):
    parts = jnp.dot(rows, split, preferred_element_type=F32)
    for c in range(4):
        for x in range(count):
            for dz in range(4):
                fine[pl.ds(x * 128 + dz * 32 + c * 8, 8), :] = parts[
                    (c * count + x) * 8 : (c * count + x + 1) * 8, dz * 128 : (dz + 1) * 128
                ]
    for x in range(count):
        win[x, 0:16, :] = jnp.zeros((16, 128), BF16)
        win[x, 144:160, :] = jnp.zeros((16, 128), BF16)
        for y in range(8):
            win[x, (y + 1) * 16 : (y + 2) * 16, :] = fine[pl.ds(x * 128 + y, 16, stride=8), :].astype(BF16)


def window(planes, y):
    return jnp.concatenate([ref[x, 32 * y : 32 * y + 64, :] for ref, x in planes], axis=0)


def first_layer(planes, w1, bias, keep_pre, keep_pooled, mask):
    lane = lax.broadcasted_iota(jnp.int32, (32, 128), 1)
    for y0 in (0, 2):
        both = jnp.concatenate([window(planes, y0), window(planes, y0 + 1)], axis=1)
        pre = jnp.dot(w1, both, preferred_element_type=F32) + bias
        if keep_pre is not None:
            for i in range(2):
                keep_pre[y0 + i] = pre[:, i * 128 : (i + 1) * 128].astype(BF16)
        act = jnp.maximum(pre, leak_slope * pre)
        total = act[0:32]
        for s in range(1, 8):
            total = total + act[s * 32 : (s + 1) * 32]
        total = mask(total * 0.125)
        for i in range(2):
            pooled = total[:, i * 128 : (i + 1) * 128]
            at = (y0 + i) * 128
            keep_pooled[at : at + 32, :] = jnp.where(lane == 0, 0.0, pltpu.roll(pooled, 1, 1)).astype(BF16)
            keep_pooled[at + 32 : at + 64, :] = pooled.astype(BF16)
            keep_pooled[at + 64 : at + 96, :] = jnp.where(lane == 127, 0.0, pltpu.roll(pooled, 127, 1)).astype(BF16)
            keep_pooled[at + 96 : at + 128, :] = jnp.ones((32, 128), BF16)


def own_kernel(
    vol_hbm, cot_hbm, w1_hbm, w2_hbm, b1_hbm, b2_hbm,
    w1big_ref, wexp_ref, wt_ref, b1_ref, b2_ref, split_ref, compact_ref, cot_out, win, pre_out, pooled_out,
    vol_ref, cot_ref, w1_ref, w2_ref, b1_row, b2_row, rows8, fine, cot_s, w2_pad, sems,
):
    sources = (vol_hbm, w1_hbm, b1_hbm, b2_hbm, w2_hbm, cot_hbm)
    targets = (vol_ref, w1_ref, b1_row, b2_row, w2_ref, cot_ref)
    copies = [pltpu.make_async_copy(x, y, sems.at[i]) for i, (x, y) in enumerate(zip(sources, targets))]
    for copy in copies:
        copy.start()
    row = lax.broadcasted_iota(jnp.int32, (108, 256), 0)
    column = lax.broadcasted_iota(jnp.int32, (108, 256), 1)
    base = row // 36 * 64 + row // 12 % 3 * 16 + row % 12
    spread = jnp.where(column == base, 1.0, 0.0).astype(BF16)
    z = lax.broadcasted_iota(jnp.int32, (256, 128), 0)
    k = lax.broadcasted_iota(jnp.int32, (256, 128), 1)
    for dz in range(4):
        split_ref[:, dz * 128 : (dz + 1) * 128] = jnp.where(z == 2 * k - 1 + dz, 1.0, 0.0).astype(BF16)
    base = k // 36 * 64 + k // 12 % 3 * 16 + k % 12
    compact_ref[...] = jnp.where((z == base) & (k < 108), 1.0, 0.0)
    rows8[...] = jnp.zeros((16, 128), F32)
    w2_pad[...] = jnp.zeros((64, 1024), F32)
    for copy in copies[:4]:
        copy.wait()

    wide = jnp.dot(w1_ref[...], spread, preferred_element_type=F32)
    for s in range(8):
        shift = cell_shift(s)
        moved = pltpu.roll(wide, shift, 1) if shift else wide
        w1big_ref[s * 32 : (s + 1) * 32, :] = moved.astype(BF16)
    rows8[0:1, 0:32] = b1_row[...]
    rows8[8:9, 0:64] = b2_row[...]
    b1 = jnp.broadcast_to(rows8[0:1, :], (128, 128)).T[:32]
    b1_ref[...] = jnp.concatenate([b1] * 8, axis=0)
    b2 = jnp.broadcast_to(rows8[8:9, :], (128, 128)).T[:64]
    b2_ref[...] = jnp.concatenate([b2] * 4, axis=0)

    rows = vol_ref[...].astype(F32).reshape(256, 256).astype(BF16)
    split_phases(rows, split_ref[...], 8, fine, win)
    bias = b1_ref[...]
    bias = jnp.concatenate([bias, bias], axis=1)
    for i in range(2):
        planes = [(win, 1 + 2 * i + dx) for dx in range(4)]
        first_layer(planes, w1big_ref[...], bias, pre_out.at[i], pooled_out.at[i], lambda v: v)

    copies[4].wait()
    w2_pad[:, 0:864] = w2_ref[...].astype(F32)
    lane = lax.broadcasted_iota(jnp.int32, (64, 128), 1)
    zero = jnp.zeros((64, 128), F32)
    units = []
    for u in range(9):
        start = 96 * u // 128 * 128
        part = w2_pad[:, start : start + 256]
        if 96 * u > start:
            part = pltpu.roll(part, 256 - (96 * u - start), 1)
        units.append(jnp.where(lane < 96, part[:, :128], 0.0))
    for dx in range(3):
        for yin in range(4):
            at = (dx * 4 + yin) * 128
            rows = []
            for y in range(4):
                dy = yin - y + 1
                rows.append(units[dx * 3 + dy] if 0 <= dy <= 2 else zero)
            for pair in range(2):
                block = jnp.concatenate(rows[2 * pair : 2 * pair + 2], axis=0)
                wexp_ref[pair * 128 : (pair + 1) * 128, at : at + 128] = block.astype(BF16)
                col = (2 - dx) * 256 + pair * 128
                wt_ref[yin * 96 : (yin + 1) * 96, col : col + 128] = block.T[:96].astype(BF16)

    copies[5].wait()
    cot_s[0:1024, :] = cot_ref[...].astype(F32).reshape(1024, 128)
    for p in range(4):
        for y in range(4):
            cot_out[p, y * 64 : (y + 1) * 64, :] = cot_s[pl.ds(p * 4 + y, 64, stride=16), :].astype(BF16)


def layers_kernel(
    other_ref, pair_ref,
    w1_ref, wexp_ref, wt_ref, b1_ref, b2_ref, split_ref, compact_ref, cot_ref, win, pre_own, pooled_own,
    act_ref, grad_ref,
    halo, fine, win_low, win_high, cot_s, ps, pre_s, g2s, act_s, act_out, sem,
    *, space, last, scale_first, scale_second,
):
    place = lax.axis_index(space)
    second = place % 2

    @pl.when(second == 0)
    def _():
        halo[0] = other_ref[...]
        halo[1] = pair_ref[...]

    @pl.when(second != 0)
    def _():
        halo[0] = pair_ref[...]
        halo[1] = other_ref[...]

    for side, target in ((0, win_low), (1, win_high)):
        rows = halo[side, 0 : 4 * HALO].astype(F32).reshape(160, 256).astype(BF16)
        split_phases(rows, split_ref[...], HALO, fine.at[side], target)

    def plane(x):
        if x < HALO:
            return win_low, x
        if x < HALO + 8:
            return win, x - HALO
        return win_high, x - HALO - 8

    bias1 = b1_ref[...]
    bias1 = jnp.concatenate([bias1, bias1], axis=1)
    bias2 = b2_ref[...]
    bias2 = jnp.concatenate([bias2, bias2], axis=1)
    for q in (0, 1, 2, 5, 6, 7):
        keep = pre_s.at[0] if q == 2 else pre_s.at[1] if q == 5 else None
        if q < 2:
            mask = lambda v: jnp.where(place > 0, v, 0.0)
        elif q > 5:
            mask = lambda v: jnp.where(place < last, v, 0.0)
        else:
            mask = lambda v: v
        first_layer([plane(2 * q + dx) for dx in range(4)], w1_ref[...], bias1, keep, ps.at[q], mask)

    def pooled(q):
        return pooled_own[q - 3] if q in (3, 4) else ps[q]

    def three(r):
        return jnp.concatenate([pooled(r), pooled(r + 1), pooled(r + 2)], axis=0)

    both = jnp.concatenate([three(r) for r in range(6)], axis=1)
    pre = jnp.dot(wexp_ref[...], both, preferred_element_type=F32) + jnp.concatenate([bias2] * 3, axis=1)
    act = jnp.maximum(pre, leak_slope * pre)
    for r in range(6):
        if 1 <= r <= 4:
            cot = cot_ref[r - 1].astype(F32)
            for y in range(4):
                act_s[pl.ds((r - 1) * 4 + y, 64, stride=16), :] = act[
                    y * 64 : (y + 1) * 64, r * 128 : (r + 1) * 128
                ]
        else:
            sent = halo[r // 5, 4 * HALO : 4 * HALO + 16].astype(F32).reshape(128, 256)
            cot_s[0:128, :] = sent[:, 0:128]
            cot_s[128:256, :] = sent[:, 128:256]
            cot = jnp.concatenate([cot_s[pl.ds(y, 64, stride=4), :] for y in range(4)], axis=0)
        own = pre[:, r * 128 : (r + 1) * 128]
        g2s[r * 256 : (r + 1) * 256, :] = jnp.where(own > 0, cot, leak_slope * cot).astype(BF16)
    act_out[...] = act_s[0:1024, :].reshape(64, 16, 128).astype(BF16)
    copy = pltpu.make_async_copy(act_out, act_ref, sem)
    copy.start()

    lane = lax.broadcasted_iota(jnp.int32, (32, 128), 1)
    ones = jnp.ones((8, 512), BF16)
    all_cells, all_cols = [], []
    q = jnp.dot(
        wt_ref[...],
        jnp.concatenate([g2s[p * 256 : (p + 3) * 256, :] for p in range(4)], axis=1),
        preferred_element_type=F32,
    )
    for p in range(4):
        pre_p = pre_own.at[p - 1] if p in (1, 2) else pre_s.at[p // 3]
        cells = []
        for y in range(4):
            taps = q[y * 96 : (y + 1) * 96, p * 128 : (p + 1) * 128] * 0.125
            g = (
                jnp.where(lane == 127, 0.0, pltpu.roll(taps[0:32], 127, 1))
                + taps[32:64]
                + jnp.where(lane == 0, 0.0, pltpu.roll(taps[64:96], 1, 1))
            )
            low = leak_slope * g
            pre = pre_p[y].astype(F32)
            cells.append(
                jnp.concatenate(
                    [jnp.where(pre[s * 32 : (s + 1) * 32] > 0, g, low) for s in range(8)], axis=0
                ).astype(BF16)
            )
        planes = [plane(2 * (p + 2) + dx) for dx in range(4)]
        cols = jnp.concatenate([window(planes, y) for y in range(4)], axis=1)
        cols = jnp.concatenate([cols, ones], axis=0)
        all_cells.append(jnp.concatenate(cells, axis=1))
        all_cols.append(cols)
    m1 = lax.dot_general(
        jnp.concatenate(all_cells, axis=1), jnp.concatenate(all_cols, axis=1), NT, preferred_element_type=F32
    )

    lane96 = lax.broadcasted_iota(jnp.int32, (96, 128), 1)
    grads = jnp.concatenate([g2s[(p + 1) * 256 : (p + 2) * 256, :] for p in range(4)], axis=1)
    folded = []
    b2_grad = None
    cols = jnp.concatenate([jnp.concatenate([pooled(p + 1 + dx) for p in range(4)], axis=1) for dx in range(3)], axis=0)
    tt = lax.dot_general(cols, grads, NT, preferred_element_type=F32)
    for dx in range(3):
        t = tt[dx * 512 : (dx + 1) * 512]
        if dx == 0:
            b2_grad = t[96:104, 0:128] + t[96:104, 128:256]
        for dy in range(3):
            sums = []
            for parity in range(2):
                total = None
                for y in (parity, parity + 2):
                    yin = y + dy - 1
                    if 0 <= yin < 4:
                        piece = t[yin * 128 : yin * 128 + 96, (y // 2) * 128 : (y // 2 + 1) * 128]
                        total = piece if total is None else total + piece
                sums.append(total)
            u = jnp.where(lane96 < 64, sums[0], sums[1])
            folded.append(u + pltpu.roll(u, 64, 1))
    folded = jnp.concatenate(folded + [jnp.zeros((160, 128), F32)], axis=0) * scale_second
    lane128 = lax.broadcasted_iota(jnp.int32, (128, 128), 1)
    for j in range(0, 8, 2):
        two = jnp.where(lane128 < 64, folded[j * 128 : (j + 1) * 128], folded[(j + 1) * 128 : (j + 2) * 128]).T
        grad_ref[j] = two[:64].astype(BF16)
        if j < 6:
            grad_ref[j + 1] = two[64:].astype(BF16)

    total = m1[0:32, 0:256]
    for s in range(1, 8):
        total = total + pltpu.roll(m1[s * 32 : (s + 1) * 32, 0:256], 256 - cell_shift(s), 1)
    w1_grad = jnp.dot(total, compact_ref[...], precision=lax.Precision.HIGHEST, preferred_element_type=F32)
    sums = m1[0:32, 256:257]
    for s in range(1, 8):
        sums = sums + m1[s * 32 : (s + 1) * 32, 256:257]
    b1_grad = jnp.concatenate([jnp.broadcast_to(sums, (32, 128)), jnp.zeros((96, 128), F32)], axis=0).T[:8]
    b2_grad = b2_grad + pltpu.roll(b2_grad, 64, 1)
    biases = jnp.concatenate([b1_grad * scale_first, b2_grad * scale_second], axis=0)
    grad_ref[7, 0:32, :] = (w1_grad * scale_first).astype(BF16)
    grad_ref[7, 32:48, :] = biases.astype(BF16)
    grad_ref[7, 48:64, :] = jnp.zeros((16, 128), BF16)
    copy.wait()


def unpack_kernel(total_ref, w1_ref, b1_ref, w2_ref, b2_ref, w1_s, b1_s, w2_s, b2_s, sems):
    rest = total_ref[7].astype(F32)
    w1_s[...] = rest[0:32, 0:108]
    b1_s[...] = rest[32:33, 0:32]
    b2_s[...] = rest[40:41, 0:64]
    copies = []

    def send(source, target):
        copies.append(pltpu.make_async_copy(source, target, sems.at[len(copies)]))
        copies[-1].start()

    send(w1_s, w1_ref)
    send(b1_s, b1_ref)
    send(b2_s, b2_ref)
    for i in range(0, 64, 16):
        for j in range(6):
            w2_s[i : i + 16, j * 128 : (j + 1) * 128] = total_ref[j, i : i + 16].astype(F32)
        w2_s[i : i + 16, 768:864] = total_ref[6, i : i + 16].astype(F32)[:, :96]
        send(w2_s.at[pl.ds(i, 16)], w2_ref.at[pl.ds(i, 16)])
    for copy in copies:
        copy.wait()


def sum_everywhere(packed):
    vmem = pl.BlockSpec(memory_space=pltpu.VMEM)
    for axes in (("x", "c"), ("yh", "yl"), "z"):
        parts = lax.all_to_all(packed, axes, 0, 0, tiled=True)
        packed = pl.pallas_call(
            add_kernel,
            out_shape=jax.ShapeDtypeStruct(packed.shape, packed.dtype),
            in_specs=[vmem],
            out_specs=vmem,
            compiler_params=pltpu.CompilerParams(vmem_limit_bytes=8 * 2**20),
            name="add",
        )(parts)
    return lax.all_to_all(packed, ("x", "c"), 0, 0, tiled=True)


def local_step(volume, w1, b1, w2, b2, cotangent, space, count, cells):
    vol, cot = volume[0], cotangent[0]
    vmem, anywhere = pl.BlockSpec(memory_space=pltpu.VMEM), pl.BlockSpec(memory_space=pl.ANY)

    def edges(*refs):
        edges_kernel(space, *refs)

    to_pair, to_other = pl.pallas_call(
        edges,
        out_shape=(jax.ShapeDtypeStruct((4 * HALO + 16, 8, 256), BF16),) * 2,
        in_specs=[anywhere] * 2,
        out_specs=(vmem, vmem),
        scratch_shapes=[pltpu.VMEM((2, 64, 4, 128), BF16), pltpu.SemaphoreType.DMA((2, 5))],
        compiler_params=pltpu.CompilerParams(vmem_limit_bytes=8 * 2**20),
        name="edges",
    )(in_hbm(vol), in_hbm(cot))
    pairs = [(i, i ^ 1) for i in range(count)]
    others = [(i, i + 1) for i in range(1, count - 1, 2)] + [(i + 1, i) for i in range(1, count - 1, 2)]
    from_other = lax.ppermute(to_other, space, others)
    from_pair = lax.ppermute(to_pair, space, pairs)
    shapes = (
        ((256, 256), BF16),
        ((256, 1536), BF16),
        ((384, 768), BF16),
        ((256, 128), F32),
        ((256, 128), F32),
        ((256, 512), BF16),
        ((256, 128), F32),
        ((4, 256, 128), BF16),
        ((8, 160, 128), BF16),
        ((2, 4, 256, 128), BF16),
        ((2, 512, 128), BF16),
    )
    inputs = [in_hbm(x) for x in (vol, cot, w1, w2, b1.reshape(1, 32), b2.reshape(1, 64))]
    own = pl.pallas_call(
        own_kernel,
        out_shape=tuple(jax.ShapeDtypeStruct(*shape) for shape in shapes),
        in_specs=[anywhere] * 6,
        out_specs=(vmem,) * len(shapes),
        scratch_shapes=[
            *(pltpu.VMEM(x.shape, x.dtype) for x in inputs),
            pltpu.VMEM((16, 128), F32),
            pltpu.VMEM((8 * 128 + 8, 128), F32),
            pltpu.VMEM((1040, 128), F32),
            pltpu.VMEM((64, 1024), F32),
            pltpu.SemaphoreType.DMA((6,)),
        ],
        compiler_params=pltpu.CompilerParams(vmem_limit_bytes=16 * 2**20),
        cost_estimate=pl.CostEstimate(flops=500_000_000, bytes_accessed=4_000_000, transcendentals=0),
        name="own_planes",
    )(*inputs)

    def kernel(*refs):
        layers_kernel(
            *refs,
            space=space,
            last=count - 1,
            scale_first=1.0 / math.sqrt(cells),
            scale_second=1.0 / math.sqrt(cells / 8.0),
        )

    act, packed = pl.pallas_call(
        kernel,
        out_shape=(
            jax.ShapeDtypeStruct((64, 16, 128), BF16),
            jax.ShapeDtypeStruct((8, 64, 128), BF16),
        ),
        in_specs=[vmem] * (2 + len(shapes)),
        out_specs=(anywhere, vmem),
        scratch_shapes=[
            pltpu.VMEM((2, 4 * HALO + 16, 8, 256), BF16),
            pltpu.VMEM((2, HALO * 128 + 8, 128), F32),
            pltpu.VMEM((HALO, 160, 128), BF16),
            pltpu.VMEM((HALO, 160, 128), BF16),
            pltpu.VMEM((264, 128), F32),
            pltpu.VMEM((8, 512, 128), BF16),
            pltpu.VMEM((2, 4, 256, 128), BF16),
            pltpu.VMEM((6 * 256, 128), BF16),
            pltpu.VMEM((1040, 128), F32),
            pltpu.VMEM((64, 16, 128), BF16),
            pltpu.SemaphoreType.DMA,
        ],
        compiler_params=pltpu.CompilerParams(vmem_limit_bytes=32 * 2**20),
        cost_estimate=pl.CostEstimate(flops=2_500_000_000, bytes_accessed=4_000_000, transcendentals=0),
        name="layers",
    )(from_other, from_pair, *own)
    return act.reshape(1, 64, 4, 4, 128), packed


def solution(mesh):
    dp, space = mesh.shape["dp"], mesh.shape["space"]
    split = Mesh(mesh.devices.reshape(8, 2, 4, 4, 2), ("z", "yh", "x", "yl", "c"))
    along = ("x", "yl", "c")

    def on_device(volume, w1, b1, w2, b2, cotangent):
        cells = float(math.prod(volume.shape[2:]) * dp * space)
        act, packed = local_step(volume, w1, b1, w2, b2, cotangent, along, space, cells)
        total = sum_everywhere(packed)
        gw1, gb1, gw2, gb2 = pl.pallas_call(
            unpack_kernel,
            out_shape=(
                jax.ShapeDtypeStruct((32, 108), F32),
                jax.ShapeDtypeStruct((1, 32), F32),
                jax.ShapeDtypeStruct((64, 864), F32),
                jax.ShapeDtypeStruct((1, 64), F32),
            ),
            in_specs=[pl.BlockSpec(memory_space=pltpu.VMEM)],
            out_specs=(pl.BlockSpec(memory_space=pl.ANY),) * 4,
            scratch_shapes=[
                pltpu.VMEM((32, 108), F32),
                pltpu.VMEM((1, 32), F32),
                pltpu.VMEM((64, 864), F32),
                pltpu.VMEM((1, 64), F32),
                pltpu.SemaphoreType.DMA((7,)),
            ],
            compiler_params=pltpu.CompilerParams(vmem_limit_bytes=8 * 2**20),
            name="unpack",
        )(total)
        return act, gw1, gb1[0], gw2, gb2[0]

    shared = P(("z", "yh"), None, along, None, None)
    return jax.shard_map(
        on_device,
        mesh=split,
        in_specs=(shared, P(), P(), P(), P(), shared),
        out_specs=(shared, P(), P(), P(), P()),
        check_vma=False,
    )
```

time: 364 us -> 70.2 us (0.19)
  waiting for transfers between devices: 103 us -> 0.01 us
  local copies, waits for them, and re-layouts: 84 us -> 0 us
  blocking collectives: 110 us -> 51.9 us
  other arithmetic: 16.8 us -> 0 us
  matrix products: 15.5 us -> 0 us
  between operations: 14.6 us -> 0.7 us
  starting transfers between devices: 19.7 us -> 9.46 us
  Pallas kernels: 0 us -> 7.74 us
    psum x1 -> x0, blocking collectives: 110 us -> none  [on_device(): lax.psum((grad_first_weight, grad_first_bias, grad_second_weight, grad_se...]
    psum x1 -> x0, waiting for transfers between devices: 100 us -> none  [on_device(): lax.psum((grad_first_weight, grad_first_bias, grad_second_weight, grad_se...]
    all_to_all x0 -> x4, blocking collectives: none -> 51.9 us  [the longest x3 40.5 us: sum_everywhere(): parts = lax.all_to_all(packed, axes, 0, 0, tiled=True)]
    unnamed x95 -> x0, local copies, waits for them, and re-layouts: 30.6 us -> none
    reshape x5 -> x0, local copies, waits for them, and re-layouts: 24.2 us -> none  [the longest x3 21.5 us: columns(): return stacked.reshape(27 * padded.shape[0], planes * height * depth)]
    dot_general x5 -> x0, matrix products: 15.5 us -> none  [the longest x1 4.38 us: on_device(): jnp.dot(flipped, stacked_back, preferred_element_type=jnp.float32)]
    reduce_sum x2 -> x0, other arithmetic: 11.1 us -> none  [the longest x1 8.83 us: avg_pool(): field.reshape(chans, planes // 2, 2, height // 2, 2, depth // 2, 2)]
    ppermute x6 -> x2, starting transfers between devices: 19.7 us -> 9.46 us  [the longest x1 4.86 us: local_step(): from_pair = lax.ppermute(to_pair, space, pairs)]
  transfers between devices with their start and end apart: 7 -> 2, of which waited for: 2 -> 0; matrix products, arithmetic and copies ran while one was open for 20% -> 0% of each run, Pallas kernels for 0% -> 3%
where the time goes in v3:
time: 70.2 us; the launch traced here: 69.8 us
  blocking collectives  51.9 us (74%)
  starting transfers between devices  9.46 us (13%)
  Pallas kernels  7.74 us (11%)
    all_to_all x3, blocking collectives, sum_everywhere(): parts = lax.all_to_all(packed, axes, 0, 0, tiled=True)  40.5 us
    all_to_all x1, blocking collectives, sum_everywhere(): return lax.all_to_all(packed, ('x', 'c'), 0, 0, tiled=True)  11.5 us
    ppermute x1, starting transfers between devices, local_step(): from_pair = lax.ppermute(to_pair, space, pairs)  4.86 us
    ppermute x1, starting transfers between devices, local_step(): from_other = lax.ppermute(to_other, space, others)  4.59 us
    pallas_call x1, Pallas kernels, local_step(): pl.pallas_call(kernel, out_shape=(jax.ShapeDtypeStruct((64, 16, 128), BF1...  3.57 us
    pallas_call x1, Pallas kernels, local_step(): pl.pallas_call(own_kernel, out_shape=tuple((jax.ShapeDtypeStruct(*shape)...  2.26 us
  transfers between devices with their start and end apart: 2, of which 0 were waited for; matrix products, arithmetic and copies ran while one was open for 0% of the time, Pallas kernels for 3%

profile of v3, /device:TPU:1, one launch (start us, length us, event | category | flops | bytes accessed | tf_op | source)
XLA Modules:
  0.0 69.8 jit_solution(14447394150083516298)
XLA Ops:
  0.6 1.1 %edges.1 = (bf16[36,8,256]{2,1,0:T(8,128)(2,1)S(1)}, bf16[36,8,256]{2,1,0:T(8,128)(2,1)S(1)}) custom-call(bf16[4,8,8,256]{3,2,1,0:T(8,128)(2,1)} %bitcast.9, bf16[64,4,4,128]{3,2,1,0:T(4,128)(2,1)} %bitcast.7), custom_call_target="tpu_custom_call" | custom-call | tf_op jit(solution)/shard_map/edges/pallas_call | solution.py:363
  1.7 4.6 %collective-permute-start = (bf16[36,8,256]{2,1,0:T(8,128)(2,1)S(1)}, bf16[36,8,256]{2,1,0:T(8,128)(2,1)S(1)}, u32[]{:S(2)}, u32[]{:S(2)}) collective-permute-start(bf16[36,8,256]{2,1,0:T(8,128)(2,1)S(1)} %get-tuple-element.24), channel_id=1, source_target_pairs={{1,2},{3,4},{5,6},{7,8},{9,10},{11,12},{13,14},{15,16},{17,18},{19... | collective-permute-start | bytes 442376 | tf_op jit(solution)/shard_map/ppermute | solution.py:374
  6.3 4.9 %collective-permute-start.1 = (bf16[36,8,256]{2,1,0:T(8,128)(2,1)S(1)}, bf16[36,8,256]{2,1,0:T(8,128)(2,1)S(1)}, u32[]{:S(2)}, u32[]{:S(2)}) collective-permute-start(bf16[36,8,256]{2,1,0:T(8,128)(2,1)S(1)} %get-tuple-element.25), channel_id=1, source_target_pairs={{0,1},{1,0},{2,3},{3,2},{4,5},{5,4},{6,7},{7,6},{8,9},{9,8},{10,11... | collective-permute-start | bytes 442376 | tf_op jit(solution)/shard_map/ppermute | solution.py:375
  11.2 2.3 %own_planes.1 = (bf16[256,256]{1,0:T(8,128)(2,1)S(1)}, bf16[256,1536]{1,0:T(8,128)(2,1)S(1)}, bf16[384,768]{1,0:T(8,128)(2,1)S(1)}, f32[256,128]{1,0:T(8,128)S(1...) custom-call(bf16[4,8,8,256]{3,2,1,0:T(8,128)(2,1)} %bitcast.10, ...), custom_call_target="tpu_custom_call" | custom-call | flops 500000000 | bytes 4000000 | tf_op jit(solution)/shard_map/own_planes/pallas_call | solution.py:390
  13.5 0.0 collective-permute-done.refs_0_
  13.5 0.0 collective-permute-done.1.refs_1_
  13.5 3.6 %layers.1 = (bf16[64,16,128]{2,1,0:T(8,128)(2,1)}, bf16[8,64,128]{2,1,0:T(8,128)(2,1)S(1)}) custom-call(bf16[36,8,256]{2,1,0:T(8,128)(2,1)S(1)} %collective-permute-done.refs_0_, bf16[36,8,256]{2,1,0:T(8,128)(2,1)S(1)} %collective-permute-done.1.refs_1_, bf16[256,256]{1,0:T(8,128)(2,1)S(1)} %get-tuple-element.26.refs_2_, ...), custom_call_target="tpu_custom_call" | custom-call | flops 2500000000 | bytes 4000000 | tf_op jit(solution)/shard_map/layers/pallas_call | solution.py:417
  17.1 9.3 %all_to_all.20.parts_ref = bf16[8,64,128]{2,1,0:T(8,128)(2,1)S(1)} all-to-all(bf16[8,64,128]{2,1,0:T(8,128)(2,1)S(1)} %get-tuple-element.38), channel_id=1, replica_groups=mesh['z'=8,'yh'=2,'x'=4,'yl'=4,'c'=2] {'x','c'}, dimensions={0} | all-to-all | bytes 262144 | tf_op jit(solution)/shard_map/all_to_all | solution.py:344
  26.4 13.4 %all_to_all.21.parts_ref = bf16[8,64,128]{2,1,0:T(8,128)(2,1)S(1)} all-to-all(bf16[8,64,128]{2,1,0:T(8,128)(2,1)S(1)} %add.3), channel_id=1, replica_groups=mesh['z'=8,'yh'=2,'x'=4,'yl'=4,'c'=2] {'yh','yl'}, dimensions={0} | all-to-all | bytes 262144 | tf_op jit(solution)/shard_map/all_to_all | solution.py:344
  39.8 17.8 %all_to_all.22.parts_ref = bf16[8,64,128]{2,1,0:T(8,128)(2,1)S(1)} all-to-all(bf16[8,64,128]{2,1,0:T(8,128)(2,1)S(1)} %add.4), channel_id=1, replica_groups=mesh['z'=8,'yh'=2,'x'=4,'yl'=4,'c'=2] {'z'}, dimensions={0} | all-to-all | bytes 262144 | tf_op jit(solution)/shard_map/all_to_all | solution.py:344
  57.6 11.5 %all_to_all.23.total_ref = bf16[8,64,128]{2,1,0:T(8,128)(2,1)S(1)} all-to-all(bf16[8,64,128]{2,1,0:T(8,128)(2,1)S(1)} %add.5), channel_id=1, replica_groups=mesh['z'=8,'yh'=2,'x'=4,'yl'=4,'c'=2] {'x','c'}, dimensions={0} | all-to-all | bytes 262144 | tf_op jit(solution)/shard_map/all_to_all | solution.py:353
  69.1 0.8 %unpack.1 = (f32[32,108]{1,0:T(8,128)}, f32[1,32]{1,0:T(1,128)}, f32[64,864]{1,0:T(8,128)}, f32[1,64]{1,0:T(1,128)}) custom-call(bf16[8,64,128]{2,1,0:T(8,128)(2,1)S(1)} %all_to_all.23.total_ref), custom_call_target="tpu_custom_call" | custom-call | tf_op jit(solution)/shard_map/unpack/pallas_call | solution.py:454
  (3 shorter events, 0.1 us)
Async XLA Ops:
  1.7 11.7 %collective-permute-start = (bf16[36,8,256]{2,1,0:T(8,128)(2,1)S(1)}, bf16[36,8,256]{2,1,0:T(8,128)(2,1)S(1)}, u32[]{:S(2)}, u32[]{:S(2)}) collective-permute-start(bf16[36,8,256]{2,1,0:T(8,128)(2,1)S(1)} %get-tuple-element.24), channel_id=1, source_target_pairs={{1,2},{3,4},{5,6},{7,8},{9,10},{11,12},{13,14},{15,16},{17,18},{19... | collective-permute-start | bytes 442376 | tf_op jit(solution)/shard_map/ppermute | solution.py:374
  6.3 7.2 %collective-permute-start.1 = (bf16[36,8,256]{2,1,0:T(8,128)(2,1)S(1)}, bf16[36,8,256]{2,1,0:T(8,128)(2,1)S(1)}, u32[]{:S(2)}, u32[]{:S(2)}) collective-permute-start(bf16[36,8,256]{2,1,0:T(8,128)(2,1)S(1)} %get-tuple-element.25), channel_id=1, source_target_pairs={{0,1},{1,0},{2,3},{3,2},{4,5},{5,4},{6,7},{7,6},{8,9},{9,8},{10,11... | collective-permute-start | bytes 442376 | tf_op jit(solution)/shard_map/ppermute | solution.py:375

commit v4 on v3

--- a/solution.py
+++ b/solution.py
@@ -12,6 +12,9 @@
 F32, BF16 = jnp.float32, jnp.bfloat16
 HALO = 5
 NT = (((1,), (1,)), ((), ()))
+BITS = ("z2", "z1", "z0", "y2", "x1", "x0", "y1", "y0", "c")
+DP, SPACE = BITS[:4], BITS[4:]
+CORES, Y, Z = ("x0", "x1", "c"), ("y0", "y1", "y2"), ("z0", "z1", "z2")
 
 
 def edges_kernel(space, vol_ref, cot_ref, pair_ref, other_ref, cot_s, sems):
@@ -340,7 +343,7 @@
 
 def sum_everywhere(packed):
     vmem = pl.BlockSpec(memory_space=pltpu.VMEM)
-    for axes in (("x", "c"), ("yh", "yl"), "z"):
+    for axes in (CORES, Y, Z):
         parts = lax.all_to_all(packed, axes, 0, 0, tiled=True)
         packed = pl.pallas_call(
             add_kernel,
@@ -350,7 +353,7 @@
             compiler_params=pltpu.CompilerParams(vmem_limit_bytes=8 * 2**20),
             name="add",
         )(parts)
-    return lax.all_to_all(packed, ("x", "c"), 0, 0, tiled=True)
+    return lax.all_to_all(packed, CORES, 0, 0, tiled=True)
 
 
 def local_step(volume, w1, b1, w2, b2, cotangent, space, count, cells):
@@ -444,12 +447,11 @@
 
 def solution(mesh):
     dp, space = mesh.shape["dp"], mesh.shape["space"]
-    split = Mesh(mesh.devices.reshape(8, 2, 4, 4, 2), ("z", "yh", "x", "yl", "c"))
-    along = ("x", "yl", "c")
+    split = Mesh(mesh.devices.reshape((2,) * 9), BITS)
 
     def on_device(volume, w1, b1, w2, b2, cotangent):
         cells = float(math.prod(volume.shape[2:]) * dp * space)
-        act, packed = local_step(volume, w1, b1, w2, b2, cotangent, along, space, cells)
+        act, packed = local_step(volume, w1, b1, w2, b2, cotangent, SPACE, space, cells)
         total = sum_everywhere(packed)
         gw1, gb1, gw2, gb2 = pl.pallas_call(
             unpack_kernel,
@@ -473,7 +475,7 @@
         )(total)
         return act, gw1, gb1[0], gw2, gb2[0]
 
-    shared = P(("z", "yh"), None, along, None, None)
+    shared = P(DP, None, SPACE, None, None)
     return jax.shard_map(
         on_device,
         mesh=split,

time: 70.2 us -> 67.9 us (0.967)
  blocking collectives: 51.9 us -> 49.6 us
    all_to_all x3, blocking collectives: 40.5 us -> 38.2 us  [sum_everywhere(): parts = lax.all_to_all(packed, axes, 0, 0, tiled=True)]
where the time goes in v4:
time: 67.9 us; the launch traced here: 67.5 us
  blocking collectives  49.6 us (73%)
  starting transfers between devices  9.46 us (14%)
  Pallas kernels  7.75 us (11%)
  between operations  0.7 us (1%)
    all_to_all x3, blocking collectives, sum_everywhere(): parts = lax.all_to_all(packed, axes, 0, 0, tiled=True)  38.2 us
    all_to_all x1, blocking collectives, sum_everywhere(): return lax.all_to_all(packed, CORES, 0, 0, tiled=True)  11.4 us
    ppermute x1, starting transfers between devices, local_step(): from_pair = lax.ppermute(to_pair, space, pairs)  4.86 us
    ppermute x1, starting transfers between devices, local_step(): from_other = lax.ppermute(to_other, space, others)  4.59 us
    pallas_call x1, Pallas kernels, local_step(): pl.pallas_call(kernel, out_shape=(jax.ShapeDtypeStruct((64, 16, 128), BF1...  3.57 us
    pallas_call x1, Pallas kernels, local_step(): pl.pallas_call(own_kernel, out_shape=tuple((jax.ShapeDtypeStruct(*shape)...  2.26 us
  transfers between devices with their start and end apart: 2, of which 0 were waited for; matrix products, arithmetic and copies ran while one was open for 0% of the time, Pallas kernels for 3%

profile of v4, /device:TPU:1, one launch (start us, length us, event | category | flops | bytes accessed | tf_op | source)
XLA Modules:
  0.0 67.5 jit_solution(2232822776427240950)
XLA Ops:
  0.6 1.1 %edges.1 = (bf16[36,8,256]{2,1,0:T(8,128)(2,1)S(1)}, bf16[36,8,256]{2,1,0:T(8,128)(2,1)S(1)}) custom-call(bf16[4,8,8,256]{3,2,1,0:T(8,128)(2,1)} %bitcast.9, bf16[64,4,4,128]{3,2,1,0:T(4,128)(2,1)} %bitcast.7), custom_call_target="tpu_custom_call" | custom-call | tf_op jit(solution)/shard_map/edges/pallas_call | solution.py:366
  1.7 4.6 %collective-permute-start = (bf16[36,8,256]{2,1,0:T(8,128)(2,1)S(1)}, bf16[36,8,256]{2,1,0:T(8,128)(2,1)S(1)}, u32[]{:S(2)}, u32[]{:S(2)}) collective-permute-start(bf16[36,8,256]{2,1,0:T(8,128)(2,1)S(1)} %get-tuple-element.24), channel_id=1, source_target_pairs={{1,2},{3,4},{5,6},{7,8},{9,10},{11,12},{13,14},{15,16},{17,18},{19... | collective-permute-start | bytes 442376 | tf_op jit(solution)/shard_map/ppermute | solution.py:377
  6.3 4.9 %collective-permute-start.1 = (bf16[36,8,256]{2,1,0:T(8,128)(2,1)S(1)}, bf16[36,8,256]{2,1,0:T(8,128)(2,1)S(1)}, u32[]{:S(2)}, u32[]{:S(2)}) collective-permute-start(bf16[36,8,256]{2,1,0:T(8,128)(2,1)S(1)} %get-tuple-element.25), channel_id=1, source_target_pairs={{0,1},{1,0},{2,3},{3,2},{4,5},{5,4},{6,7},{7,6},{8,9},{9,8},{10,11... | collective-permute-start | bytes 442376 | tf_op jit(solution)/shard_map/ppermute | solution.py:378
  11.2 2.3 %own_planes.1 = (bf16[256,256]{1,0:T(8,128)(2,1)S(1)}, bf16[256,1536]{1,0:T(8,128)(2,1)S(1)}, bf16[384,768]{1,0:T(8,128)(2,1)S(1)}, f32[256,128]{1,0:T(8,128)S(1...) custom-call(bf16[4,8,8,256]{3,2,1,0:T(8,128)(2,1)} %bitcast.10, ...), custom_call_target="tpu_custom_call" | custom-call | flops 500000000 | bytes 4000000 | tf_op jit(solution)/shard_map/own_planes/pallas_call | solution.py:393
  13.5 0.0 collective-permute-done.refs_0_
  13.5 0.0 collective-permute-done.1.refs_1_
  13.5 3.6 %layers.1 = (bf16[64,16,128]{2,1,0:T(8,128)(2,1)}, bf16[8,64,128]{2,1,0:T(8,128)(2,1)S(1)}) custom-call(bf16[36,8,256]{2,1,0:T(8,128)(2,1)S(1)} %collective-permute-done.refs_0_, bf16[36,8,256]{2,1,0:T(8,128)(2,1)S(1)} %collective-permute-done.1.refs_1_, bf16[256,256]{1,0:T(8,128)(2,1)S(1)} %get-tuple-element.26.refs_2_, ...), custom_call_target="tpu_custom_call" | custom-call | flops 2500000000 | bytes 4000000 | tf_op jit(solution)/shard_map/layers/pallas_call | solution.py:420
  17.1 9.3 %all_to_all.20.parts_ref = bf16[8,64,128]{2,1,0:T(8,128)(2,1)S(1)} all-to-all(bf16[8,64,128]{2,1,0:T(8,128)(2,1)S(1)} %get-tuple-element.38), channel_id=1, replica_groups=mesh['z2'=2,'z1'=2,'z0'=2,'y2'=2,'x1'=2,'x0'=2,'y1'=2,'y0'=2,'c'=2] {'x0..., dimensions={0} | all-to-all | bytes 262144 | tf_op jit(solution)/shard_map/all_to_all | solution.py:347
  26.4 12.4 %all_to_all.21.parts_ref = bf16[8,64,128]{2,1,0:T(8,128)(2,1)S(1)} all-to-all(bf16[8,64,128]{2,1,0:T(8,128)(2,1)S(1)} %add.3), channel_id=1, replica_groups=mesh['z2'=2,'z1'=2,'z0'=2,'y2'=2,'x1'=2,'x0'=2,'y1'=2,'y0'=2,'c'=2] {'y0..., dimensions={0} | all-to-all | bytes 262144 | tf_op jit(solution)/shard_map/all_to_all | solution.py:347
  38.8 16.6 %all_to_all.22.parts_ref = bf16[8,64,128]{2,1,0:T(8,128)(2,1)S(1)} all-to-all(bf16[8,64,128]{2,1,0:T(8,128)(2,1)S(1)} %add.4), channel_id=1, replica_groups=mesh['z2'=2,'z1'=2,'z0'=2,'y2'=2,'x1'=2,'x0'=2,'y1'=2,'y0'=2,'c'=2] {'z0..., dimensions={0} | all-to-all | bytes 262144 | tf_op jit(solution)/shard_map/all_to_all | solution.py:347
  55.4 11.4 %all_to_all.23.total_ref = bf16[8,64,128]{2,1,0:T(8,128)(2,1)S(1)} all-to-all(bf16[8,64,128]{2,1,0:T(8,128)(2,1)S(1)} %add.5), channel_id=1, replica_groups=mesh['z2'=2,'z1'=2,'z0'=2,'y2'=2,'x1'=2,'x0'=2,'y1'=2,'y0'=2,'c'=2] {'x0..., dimensions={0} | all-to-all | bytes 262144 | tf_op jit(solution)/shard_map/all_to_all | solution.py:356
  66.8 0.8 %unpack.1 = (f32[32,108]{1,0:T(8,128)}, f32[1,32]{1,0:T(1,128)}, f32[64,864]{1,0:T(8,128)}, f32[1,64]{1,0:T(1,128)}) custom-call(bf16[8,64,128]{2,1,0:T(8,128)(2,1)S(1)} %all_to_all.23.total_ref), custom_call_target="tpu_custom_call" | custom-call | tf_op jit(solution)/shard_map/unpack/pallas_call | solution.py:456
  (3 shorter events, 0.1 us)
Async XLA Ops:
  1.7 11.7 %collective-permute-start = (bf16[36,8,256]{2,1,0:T(8,128)(2,1)S(1)}, bf16[36,8,256]{2,1,0:T(8,128)(2,1)S(1)}, u32[]{:S(2)}, u32[]{:S(2)}) collective-permute-start(bf16[36,8,256]{2,1,0:T(8,128)(2,1)S(1)} %get-tuple-element.24), channel_id=1, source_target_pairs={{1,2},{3,4},{5,6},{7,8},{9,10},{11,12},{13,14},{15,16},{17,18},{19... | collective-permute-start | bytes 442376 | tf_op jit(solution)/shard_map/ppermute | solution.py:377
  6.3 7.2 %collective-permute-start.1 = (bf16[36,8,256]{2,1,0:T(8,128)(2,1)S(1)}, bf16[36,8,256]{2,1,0:T(8,128)(2,1)S(1)}, u32[]{:S(2)}, u32[]{:S(2)}) collective-permute-start(bf16[36,8,256]{2,1,0:T(8,128)(2,1)S(1)} %get-tuple-element.25), channel_id=1, source_target_pairs={{0,1},{1,0},{2,3},{3,2},{4,5},{5,4},{6,7},{7,6},{8,9},{9,8},{10,11... | collective-permute-start | bytes 442376 | tf_op jit(solution)/shard_map/ppermute | solution.py:378

commit v5 on v4

--- a/solution.py
+++ b/solution.py
@@ -17,16 +17,30 @@
 CORES, Y, Z = ("x0", "x1", "c"), ("y0", "y1", "y2"), ("z0", "z1", "z2")
 
 
-def edges_kernel(space, vol_ref, cot_ref, pair_ref, other_ref, cot_s, sems):
+def edges_kernel(
+    space, vol_hbm, cot_hbm, pair_ref, other_ref, split_ref, compact_ref, spread_ref, cot_s, sems
+):
     second = lax.axis_index(space) % 2
     copies = []
     for side, ref, high in ((0, other_ref, second), (1, pair_ref, 1 - second)):
-        copies.append(pltpu.make_async_copy(cot_ref.at[:, high * 3], cot_s.at[side], sems.at[side, 4]))
+        copies.append(pltpu.make_async_copy(cot_hbm.at[:, high * 3], cot_s.at[side], sems.at[side, 4]))
         for c in range(4):
-            source = vol_ref.at[c, pl.ds(high * (8 - HALO), HALO)]
+            source = vol_hbm.at[c, pl.ds(high * (8 - HALO), HALO)]
             copies.append(pltpu.make_async_copy(source, ref.at[pl.ds(c * HALO, HALO)], sems.at[side, c]))
     for copy in copies:
         copy.start()
+
+    z = lax.broadcasted_iota(jnp.int32, (256, 128), 0)
+    k = lax.broadcasted_iota(jnp.int32, (256, 128), 1)
+    for dz in range(4):
+        split_ref[:, dz * 128 : (dz + 1) * 128] = jnp.where(z == 2 * k - 1 + dz, 1.0, 0.0).astype(BF16)
+    base = k // 36 * 64 + k // 12 % 3 * 16 + k % 12
+    compact_ref[...] = jnp.where((z == base) & (k < 108), 1.0, 0.0)
+    row = lax.broadcasted_iota(jnp.int32, (108, 256), 0)
+    column = lax.broadcasted_iota(jnp.int32, (108, 256), 1)
+    base = row // 36 * 64 + row // 12 % 3 * 16 + row % 12
+    spread_ref[...] = jnp.where(column == base, 1.0, 0.0).astype(BF16)
+
     for copy in copies:
         copy.wait()
     for side, ref in ((0, other_ref), (1, pair_ref)):
@@ -83,39 +97,28 @@
         total = mask(total * 0.125)
         for i in range(2):
             pooled = total[:, i * 128 : (i + 1) * 128]
-            at = (y0 + i) * 128
+            at = (y0 + i) * 96
             keep_pooled[at : at + 32, :] = jnp.where(lane == 0, 0.0, pltpu.roll(pooled, 1, 1)).astype(BF16)
             keep_pooled[at + 32 : at + 64, :] = pooled.astype(BF16)
             keep_pooled[at + 64 : at + 96, :] = jnp.where(lane == 127, 0.0, pltpu.roll(pooled, 127, 1)).astype(BF16)
-            keep_pooled[at + 96 : at + 128, :] = jnp.ones((32, 128), BF16)
 
 
 def own_kernel(
-    vol_hbm, cot_hbm, w1_hbm, w2_hbm, b1_hbm, b2_hbm,
-    w1big_ref, wexp_ref, wt_ref, b1_ref, b2_ref, split_ref, compact_ref, cot_out, win, pre_out, pooled_out,
-    vol_ref, cot_ref, w1_ref, w2_ref, b1_row, b2_row, rows8, fine, cot_s, w2_pad, sems,
+    vol_hbm, w1_hbm, b1_hbm, b2_hbm, w2_hbm, cot_hbm, split_ref, spread_ref,
+    w1big_ref, wexp_ref, wt_ref, b1_ref, b2_ref, cot_out, win, pre_out, pooled_out,
+    vol_ref, w1_ref, b1_row, b2_row, w2_ref, cot_ref, rows8, fine, cot_s, w2_pad, sems,
 ):
     sources = (vol_hbm, w1_hbm, b1_hbm, b2_hbm, w2_hbm, cot_hbm)
     targets = (vol_ref, w1_ref, b1_row, b2_row, w2_ref, cot_ref)
     copies = [pltpu.make_async_copy(x, y, sems.at[i]) for i, (x, y) in enumerate(zip(sources, targets))]
     for copy in copies:
         copy.start()
-    row = lax.broadcasted_iota(jnp.int32, (108, 256), 0)
-    column = lax.broadcasted_iota(jnp.int32, (108, 256), 1)
-    base = row // 36 * 64 + row // 12 % 3 * 16 + row % 12
-    spread = jnp.where(column == base, 1.0, 0.0).astype(BF16)
-    z = lax.broadcasted_iota(jnp.int32, (256, 128), 0)
-    k = lax.broadcasted_iota(jnp.int32, (256, 128), 1)
-    for dz in range(4):
-        split_ref[:, dz * 128 : (dz + 1) * 128] = jnp.where(z == 2 * k - 1 + dz, 1.0, 0.0).astype(BF16)
-    base = k // 36 * 64 + k // 12 % 3 * 16 + k % 12
-    compact_ref[...] = jnp.where((z == base) & (k < 108), 1.0, 0.0)
     rows8[...] = jnp.zeros((16, 128), F32)
     w2_pad[...] = jnp.zeros((64, 1024), F32)
-    for copy in copies[:4]:
+    for copy in copies:
         copy.wait()
 
-    wide = jnp.dot(w1_ref[...], spread, preferred_element_type=F32)
+    wide = jnp.dot(w1_ref[...], spread_ref[...], preferred_element_type=F32)
     for s in range(8):
         shift = cell_shift(s)
         moved = pltpu.roll(wide, shift, 1) if shift else wide
@@ -135,31 +138,23 @@
         planes = [(win, 1 + 2 * i + dx) for dx in range(4)]
         first_layer(planes, w1big_ref[...], bias, pre_out.at[i], pooled_out.at[i], lambda v: v)
 
-    copies[4].wait()
     w2_pad[:, 0:864] = w2_ref[...].astype(F32)
-    lane = lax.broadcasted_iota(jnp.int32, (64, 128), 1)
-    zero = jnp.zeros((64, 128), F32)
-    units = []
-    for u in range(9):
-        start = 96 * u // 128 * 128
-        part = w2_pad[:, start : start + 256]
-        if 96 * u > start:
-            part = pltpu.roll(part, 256 - (96 * u - start), 1)
-        units.append(jnp.where(lane < 96, part[:, :128], 0.0))
+    lane = lax.broadcasted_iota(jnp.int32, (64, 512), 1)
     for dx in range(3):
-        for yin in range(4):
-            at = (dx * 4 + yin) * 128
-            rows = []
-            for y in range(4):
-                dy = yin - y + 1
-                rows.append(units[dx * 3 + dy] if 0 <= dy <= 2 else zero)
-            for pair in range(2):
-                block = jnp.concatenate(rows[2 * pair : 2 * pair + 2], axis=0)
-                wexp_ref[pair * 128 : (pair + 1) * 128, at : at + 128] = block.astype(BF16)
-                col = (2 - dx) * 256 + pair * 128
-                wt_ref[yin * 96 : (yin + 1) * 96, col : col + 128] = block.T[:96].astype(BF16)
-
-    copies[5].wait()
+        start = dx * 288 // 128 * 128
+        taps = w2_pad[:, start : start + 512]
+        rows = []
+        for y in range(4):
+            at = 96 * (y - 1)
+            shift = (at - (dx * 288 - start)) % 512
+            moved = pltpu.roll(taps, shift, 1) if shift else taps
+            rows.append(jnp.where((lane >= max(at, 0)) & (lane < min(at + 288, 384)), moved, 0.0)[:, :384])
+        for pair in range(2):
+            block = jnp.concatenate(rows[2 * pair : 2 * pair + 2], axis=0)
+            wexp_ref[pair * 128 : (pair + 1) * 128, dx * 384 : (dx + 1) * 384] = block.astype(BF16)
+            col = (2 - dx) * 256 + pair * 128
+            wt_ref[:, col : col + 128] = block.T.astype(BF16)
+
     cot_s[0:1024, :] = cot_ref[...].astype(F32).reshape(1024, 128)
     for p in range(4):
         for y in range(4):
@@ -168,27 +163,21 @@
 
 def layers_kernel(
     other_ref, pair_ref,
-    w1_ref, wexp_ref, wt_ref, b1_ref, b2_ref, split_ref, compact_ref, cot_ref, win, pre_own, pooled_own,
+    split_ref, compact_ref, w1_ref, wexp_ref, wt_ref, b1_ref, b2_ref, cot_ref, win, pre_own, pooled_own,
     act_ref, grad_ref,
-    halo, fine, win_low, win_high, cot_s, ps, pre_s, g2s, act_s, act_out, sem,
+    fine, win_low, win_high, cot_s, ps, pre_s, g2s, act_s, act_out, sem,
     *, space, last, scale_first, scale_second,
 ):
     place = lax.axis_index(space)
     second = place % 2
 
-    @pl.when(second == 0)
-    def _():
-        halo[0] = other_ref[...]
-        halo[1] = pair_ref[...]
-
-    @pl.when(second != 0)
-    def _():
-        halo[0] = pair_ref[...]
-        halo[1] = other_ref[...]
-
-    for side, target in ((0, win_low), (1, win_high)):
-        rows = halo[side, 0 : 4 * HALO].astype(F32).reshape(160, 256).astype(BF16)
-        split_phases(rows, split_ref[...], HALO, fine.at[side], target)
+    def side(low, start, stop):
+        first, other = (other_ref, pair_ref) if low else (pair_ref, other_ref)
+        return jnp.where(second == 0, first[start:stop].astype(F32), other[start:stop].astype(F32))
+
+    for low, target in ((True, win_low), (False, win_high)):
+        rows = side(low, 0, 4 * HALO).reshape(160, 256).astype(BF16)
+        split_phases(rows, split_ref[...], HALO, fine.at[1 - low], target)
 
     def plane(x):
         if x < HALO:
@@ -228,7 +217,7 @@
                     y * 64 : (y + 1) * 64, r * 128 : (r + 1) * 128
                 ]
         else:
-            sent = halo[r // 5, 4 * HALO : 4 * HALO + 16].astype(F32).reshape(128, 256)
+            sent = side(r == 0, 4 * HALO, 4 * HALO + 16).reshape(128, 256)
             cot_s[0:128, :] = sent[:, 0:128]
             cot_s[128:256, :] = sent[:, 128:256]
             cot = jnp.concatenate([cot_s[pl.ds(y, 64, stride=4), :] for y in range(4)], axis=0)
@@ -275,13 +264,11 @@
     lane96 = lax.broadcasted_iota(jnp.int32, (96, 128), 1)
     grads = jnp.concatenate([g2s[(p + 1) * 256 : (p + 2) * 256, :] for p in range(4)], axis=1)
     folded = []
-    b2_grad = None
-    cols = jnp.concatenate([jnp.concatenate([pooled(p + 1 + dx) for p in range(4)], axis=1) for dx in range(3)], axis=0)
-    tt = lax.dot_general(cols, grads, NT, preferred_element_type=F32)
+    cols = [jnp.concatenate([pooled(p + 1 + dx) for p in range(4)], axis=1) for dx in range(3)]
+    tt = lax.dot_general(jnp.concatenate(cols + [ones], axis=0), grads, NT, preferred_element_type=F32)
+    b2_grad = tt[1152:1160, 0:128] + tt[1152:1160, 128:256]
     for dx in range(3):
-        t = tt[dx * 512 : (dx + 1) * 512]
-        if dx == 0:
-            b2_grad = t[96:104, 0:128] + t[96:104, 128:256]
+        t = tt[dx * 384 : (dx + 1) * 384]
         for dy in range(3):
             sums = []
             for parity in range(2):
@@ -289,7 +276,7 @@
                 for y in (parity, parity + 2):
                     yin = y + dy - 1
                     if 0 <= yin < 4:
-                        piece = t[yin * 128 : yin * 128 + 96, (y // 2) * 128 : (y // 2 + 1) * 128]
+                        piece = t[yin * 96 : (yin + 1) * 96, (y // 2) * 128 : (y // 2 + 1) * 128]
                         total = piece if total is None else total + piece
                 sums.append(total)
             u = jnp.where(lane96 < 64, sums[0], sums[1])
@@ -363,37 +350,42 @@
     def edges(*refs):
         edges_kernel(space, *refs)
 
-    to_pair, to_other = pl.pallas_call(
+    inputs = [in_hbm(x) for x in (vol, w1, b1.reshape(1, 32), b2.reshape(1, 64), w2, cot)]
+    message = jax.ShapeDtypeStruct((4 * HALO + 16, 8, 256), BF16)
+    to_pair, to_other, split, compact, spread = pl.pallas_call(
         edges,
-        out_shape=(jax.ShapeDtypeStruct((4 * HALO + 16, 8, 256), BF16),) * 2,
+        out_shape=(
+            message,
+            message,
+            jax.ShapeDtypeStruct((256, 512), BF16),
+            jax.ShapeDtypeStruct((256, 128), F32),
+            jax.ShapeDtypeStruct((108, 256), BF16),
+        ),
         in_specs=[anywhere] * 2,
-        out_specs=(vmem, vmem),
+        out_specs=(vmem,) * 5,
         scratch_shapes=[pltpu.VMEM((2, 64, 4, 128), BF16), pltpu.SemaphoreType.DMA((2, 5))],
         compiler_params=pltpu.CompilerParams(vmem_limit_bytes=8 * 2**20),
         name="edges",
-    )(in_hbm(vol), in_hbm(cot))
+    )(inputs[0], inputs[-1])
     pairs = [(i, i ^ 1) for i in range(count)]
     others = [(i, i + 1) for i in range(1, count - 1, 2)] + [(i + 1, i) for i in range(1, count - 1, 2)]
     from_other = lax.ppermute(to_other, space, others)
     from_pair = lax.ppermute(to_pair, space, pairs)
     shapes = (
         ((256, 256), BF16),
-        ((256, 1536), BF16),
+        ((256, 1152), BF16),
         ((384, 768), BF16),
         ((256, 128), F32),
-        ((256, 128), F32),
-        ((256, 512), BF16),
         ((256, 128), F32),
         ((4, 256, 128), BF16),
         ((8, 160, 128), BF16),
         ((2, 4, 256, 128), BF16),
-        ((2, 512, 128), BF16),
+        ((2, 384, 128), BF16),
     )
-    inputs = [in_hbm(x) for x in (vol, cot, w1, w2, b1.reshape(1, 32), b2.reshape(1, 64))]
     own = pl.pallas_call(
         own_kernel,
         out_shape=tuple(jax.ShapeDtypeStruct(*shape) for shape in shapes),
-        in_specs=[anywhere] * 6,
+        in_specs=[anywhere] * 6 + [vmem] * 2,
         out_specs=(vmem,) * len(shapes),
         scratch_shapes=[
             *(pltpu.VMEM(x.shape, x.dtype) for x in inputs),
@@ -406,7 +398,7 @@
         compiler_params=pltpu.CompilerParams(vmem_limit_bytes=16 * 2**20),
         cost_estimate=pl.CostEstimate(flops=500_000_000, bytes_accessed=4_000_000, transcendentals=0),
         name="own_planes",
-    )(*inputs)
+    )(*inputs, split, spread)
 
     def kernel(*refs):
         layers_kernel(
@@ -423,15 +415,14 @@
             jax.ShapeDtypeStruct((64, 16, 128), BF16),
             jax.ShapeDtypeStruct((8, 64, 128), BF16),
         ),
-        in_specs=[vmem] * (2 + len(shapes)),
+        in_specs=[vmem] * (4 + len(shapes)),
         out_specs=(anywhere, vmem),
         scratch_shapes=[
-            pltpu.VMEM((2, 4 * HALO + 16, 8, 256), BF16),
             pltpu.VMEM((2, HALO * 128 + 8, 128), F32),
             pltpu.VMEM((HALO, 160, 128), BF16),
             pltpu.VMEM((HALO, 160, 128), BF16),
             pltpu.VMEM((264, 128), F32),
-            pltpu.VMEM((8, 512, 128), BF16),
+            pltpu.VMEM((8, 384, 128), BF16),
             pltpu.VMEM((2, 4, 256, 128), BF16),
             pltpu.VMEM((6 * 256, 128), BF16),
             pltpu.VMEM((1040, 128), F32),
@@ -441,7 +432,7 @@
         compiler_params=pltpu.CompilerParams(vmem_limit_bytes=32 * 2**20),
         cost_estimate=pl.CostEstimate(flops=2_500_000_000, bytes_accessed=4_000_000, transcendentals=0),
         name="layers",
-    )(from_other, from_pair, *own)
+    )(from_other, from_pair, split, compact, *own)
     return act.reshape(1, 64, 4, 4, 128), packed
 
 

time: 67.9 us -> 67.8 us (level)
  no operation moved by 1% of the time
where the time goes in v5:
time: 67.8 us; the launch traced here: 67.4 us
  blocking collectives  49.5 us (73%)
  starting transfers between devices  9.46 us (14%)
  Pallas kernels  7.73 us (11%)
  between operations  0.7 us (1%)
    all_to_all x3, blocking collectives, sum_everywhere(): parts = lax.all_to_all(packed, axes, 0, 0, tiled=True)  38.2 us
    all_to_all x1, blocking collectives, sum_everywhere(): return lax.all_to_all(packed, CORES, 0, 0, tiled=True)  11.4 us
    ppermute x1, starting transfers between devices, local_step(): from_pair = lax.ppermute(to_pair, space, pairs)  4.86 us
    ppermute x1, starting transfers between devices, local_step(): from_other = lax.ppermute(to_other, space, others)  4.59 us
    pallas_call x1, Pallas kernels, local_step(): pl.pallas_call(kernel, out_shape=(jax.ShapeDtypeStruct((64, 16, 128), BF1...  3.47 us
    pallas_call x1, Pallas kernels, local_step(): pl.pallas_call(own_kernel, out_shape=tuple((jax.ShapeDtypeStruct(*shape)...  2.33 us
  transfers between devices with their start and end apart: 2, of which 0 were waited for; matrix products, arithmetic and copies ran while one was open for 0% of the time, Pallas kernels for 3%

profile of v5, /device:TPU:1, one launch (start us, length us, event | category | flops | bytes accessed | tf_op | source)
XLA Modules:
  0.0 67.4 jit_solution(17604570504005786945)
XLA Ops:
  0.6 1.1 %edges.1 = (bf16[36,8,256]{2,1,0:T(8,128)(2,1)S(1)}, bf16[36,8,256]{2,1,0:T(8,128)(2,1)S(1)}, bf16[256,512]{1,0:T(8,128)(2,1)S(1)}, f32[256,128]{1,0:T(8,128)S(1)}, bf16[108,256]{1,0:T(8,128)(2,1)S(1)}) custom-call(bf16[4,8,8,256]{3,2,1,0:T(8,128)(2,1)} %bitcast.9, bf16[64,4,4,128]{3,2,1,0:T(4,128)(2,1)} %bitcast.7), custom_call_target="tpu_custom_call" | custom-call | tf_op jit(solution)/shard_map/edges/pallas_call | solution.py:355
  1.7 4.6 %collective-permute-start = (bf16[36,8,256]{2,1,0:T(8,128)(2,1)S(1)}, bf16[36,8,256]{2,1,0:T(8,128)(2,1)S(1)}, u32[]{:S(2)}, u32[]{:S(2)}) collective-permute-start(bf16[36,8,256]{2,1,0:T(8,128)(2,1)S(1)} %get-tuple-element.25), channel_id=1, source_target_pairs={{1,2},{3,4},{5,6},{7,8},{9,10},{11,12},{13,14},{15,16},{17,18},{19... | collective-permute-start | bytes 442376 | tf_op jit(solution)/shard_map/ppermute | solution.py:372
  6.3 4.9 %collective-permute-start.1 = (bf16[36,8,256]{2,1,0:T(8,128)(2,1)S(1)}, bf16[36,8,256]{2,1,0:T(8,128)(2,1)S(1)}, u32[]{:S(2)}, u32[]{:S(2)}) collective-permute-start(bf16[36,8,256]{2,1,0:T(8,128)(2,1)S(1)} %get-tuple-element.26), channel_id=1, source_target_pairs={{0,1},{1,0},{2,3},{3,2},{4,5},{5,4},{6,7},{7,6},{8,9},{9,8},{10,11... | collective-permute-start | bytes 442376 | tf_op jit(solution)/shard_map/ppermute | solution.py:373
  11.2 2.3 %own_planes.1 = (bf16[256,256]{1,0:T(8,128)(2,1)S(1)}, bf16[256,1152]{1,0:T(8,128)(2,1)S(1)}, bf16[384,768]{1,0:T(8,128)(2,1)S(1)}, f32[256,128]{1,0:T(8,128)S(1...) custom-call(bf16[4,8,8,256]{3,2,1,0:T(8,128)(2,1)} %bitcast.10, ...), custom_call_target="tpu_custom_call" | custom-call | flops 500000000 | bytes 4000000 | tf_op jit(solution)/shard_map/own_planes/pallas_call | solution.py:385
  13.6 0.0 collective-permute-done.refs_0_
  13.6 0.0 collective-permute-done.1.refs_1_
  13.6 3.5 %layers.1 = (bf16[64,16,128]{2,1,0:T(8,128)(2,1)}, bf16[8,64,128]{2,1,0:T(8,128)(2,1)S(1)}) custom-call(bf16[36,8,256]{2,1,0:T(8,128)(2,1)S(1)} %collective-permute-done.refs_0_, bf16[36,8,256]{2,1,0:T(8,128)(2,1)S(1)} %collective-permute-done.1.refs_1_, bf16[256,512]{1,0:T(8,128)(2,1)S(1)} %get-tuple-element.27.split_ref.refs_2_, ...), custom_call_target="tpu_custom_call" | custom-call | flops 2500000000 | bytes 4000000 | tf_op jit(solution)/shard_map/layers/pallas_call | solution.py:412
  17.0 9.2 %all_to_all.20.parts_ref = bf16[8,64,128]{2,1,0:T(8,128)(2,1)S(1)} all-to-all(bf16[8,64,128]{2,1,0:T(8,128)(2,1)S(1)} %get-tuple-element.40), channel_id=1, replica_groups=mesh['z2'=2,'z1'=2,'z0'=2,'y2'=2,'x1'=2,'x0'=2,'y1'=2,'y0'=2,'c'=2] {'x0..., dimensions={0} | all-to-all | bytes 262144 | tf_op jit(solution)/shard_map/all_to_all | solution.py:334
  26.3 12.4 %all_to_all.21.parts_ref = bf16[8,64,128]{2,1,0:T(8,128)(2,1)S(1)} all-to-all(bf16[8,64,128]{2,1,0:T(8,128)(2,1)S(1)} %add.3), channel_id=1, replica_groups=mesh['z2'=2,'z1'=2,'z0'=2,'y2'=2,'x1'=2,'x0'=2,'y1'=2,'y0'=2,'c'=2] {'y0..., dimensions={0} | all-to-all | bytes 262144 | tf_op jit(solution)/shard_map/all_to_all | solution.py:334
  38.7 16.5 %all_to_all.22.parts_ref = bf16[8,64,128]{2,1,0:T(8,128)(2,1)S(1)} all-to-all(bf16[8,64,128]{2,1,0:T(8,128)(2,1)S(1)} %add.4), channel_id=1, replica_groups=mesh['z2'=2,'z1'=2,'z0'=2,'y2'=2,'x1'=2,'x0'=2,'y1'=2,'y0'=2,'c'=2] {'z0..., dimensions={0} | all-to-all | bytes 262144 | tf_op jit(solution)/shard_map/all_to_all | solution.py:334
  55.3 11.4 %all_to_all.23.total_ref = bf16[8,64,128]{2,1,0:T(8,128)(2,1)S(1)} all-to-all(bf16[8,64,128]{2,1,0:T(8,128)(2,1)S(1)} %add.5), channel_id=1, replica_groups=mesh['z2'=2,'z1'=2,'z0'=2,'y2'=2,'x1'=2,'x0'=2,'y1'=2,'y0'=2,'c'=2] {'x0..., dimensions={0} | all-to-all | bytes 262144 | tf_op jit(solution)/shard_map/all_to_all | solution.py:343
  66.7 0.8 %unpack.1 = (f32[32,108]{1,0:T(8,128)}, f32[1,32]{1,0:T(1,128)}, f32[64,864]{1,0:T(8,128)}, f32[1,64]{1,0:T(1,128)}) custom-call(bf16[8,64,128]{2,1,0:T(8,128)(2,1)S(1)} %all_to_all.23.total_ref), custom_call_target="tpu_custom_call" | custom-call | tf_op jit(solution)/shard_map/unpack/pallas_call | solution.py:447
  (3 shorter events, 0.1 us)
Async XLA Ops:
  1.7 11.8 %collective-permute-start = (bf16[36,8,256]{2,1,0:T(8,128)(2,1)S(1)}, bf16[36,8,256]{2,1,0:T(8,128)(2,1)S(1)}, u32[]{:S(2)}, u32[]{:S(2)}) collective-permute-start(bf16[36,8,256]{2,1,0:T(8,128)(2,1)S(1)} %get-tuple-element.25), channel_id=1, source_target_pairs={{1,2},{3,4},{5,6},{7,8},{9,10},{11,12},{13,14},{15,16},{17,18},{19... | collective-permute-start | bytes 442376 | tf_op jit(solution)/shard_map/ppermute | solution.py:372
  6.3 7.2 %collective-permute-start.1 = (bf16[36,8,256]{2,1,0:T(8,128)(2,1)S(1)}, bf16[36,8,256]{2,1,0:T(8,128)(2,1)S(1)}, u32[]{:S(2)}, u32[]{:S(2)}) collective-permute-start(bf16[36,8,256]{2,1,0:T(8,128)(2,1)S(1)} %get-tuple-element.26), channel_id=1, source_target_pairs={{0,1},{1,0},{2,3},{3,2},{4,5},{5,4},{6,7},{7,6},{8,9},{9,8},{10,11... | collective-permute-start | bytes 442376 | tf_op jit(solution)/shard_map/ppermute | solution.py:373

commit v6 on v5

--- a/solution.py
+++ b/solution.py
@@ -104,20 +104,25 @@
 
 
 def own_kernel(
-    vol_hbm, w1_hbm, b1_hbm, b2_hbm, w2_hbm, cot_hbm, split_ref, spread_ref,
+    w1_hbm, b1_hbm, b2_hbm, w2_hbm, vol_ref, cot_ref, split_ref, spread_ref,
     w1big_ref, wexp_ref, wt_ref, b1_ref, b2_ref, cot_out, win, pre_out, pooled_out,
-    vol_ref, w1_ref, b1_row, b2_row, w2_ref, cot_ref, rows8, fine, cot_s, w2_pad, sems,
+    w1_ref, b1_row, b2_row, w2_ref, rows8, fine, cot_s, w2_pad, sems,
 ):
-    sources = (vol_hbm, w1_hbm, b1_hbm, b2_hbm, w2_hbm, cot_hbm)
-    targets = (vol_ref, w1_ref, b1_row, b2_row, w2_ref, cot_ref)
+    sources, targets = (w1_hbm, b1_hbm, b2_hbm, w2_hbm), (w1_ref, b1_row, b2_row, w2_ref)
     copies = [pltpu.make_async_copy(x, y, sems.at[i]) for i, (x, y) in enumerate(zip(sources, targets))]
     for copy in copies:
         copy.start()
     rows8[...] = jnp.zeros((16, 128), F32)
     w2_pad[...] = jnp.zeros((64, 1024), F32)
+    rows = vol_ref[...].astype(F32).reshape(256, 256).astype(BF16)
+    split_phases(rows, split_ref[...], 8, fine, win)
+    cot_s[0:1024, :] = cot_ref[...].astype(F32).reshape(1024, 128)
+    for p in range(4):
+        for y in range(4):
+            cot_out[p, y * 64 : (y + 1) * 64, :] = cot_s[pl.ds(p * 4 + y, 64, stride=16), :].astype(BF16)
+
     for copy in copies:
         copy.wait()
-
     wide = jnp.dot(w1_ref[...], spread_ref[...], preferred_element_type=F32)
     for s in range(8):
         shift = cell_shift(s)
@@ -129,9 +134,6 @@
     b1_ref[...] = jnp.concatenate([b1] * 8, axis=0)
     b2 = jnp.broadcast_to(rows8[8:9, :], (128, 128)).T[:64]
     b2_ref[...] = jnp.concatenate([b2] * 4, axis=0)
-
-    rows = vol_ref[...].astype(F32).reshape(256, 256).astype(BF16)
-    split_phases(rows, split_ref[...], 8, fine, win)
     bias = b1_ref[...]
     bias = jnp.concatenate([bias, bias], axis=1)
     for i in range(2):
@@ -154,11 +156,6 @@
             wexp_ref[pair * 128 : (pair + 1) * 128, dx * 384 : (dx + 1) * 384] = block.astype(BF16)
             col = (2 - dx) * 256 + pair * 128
             wt_ref[:, col : col + 128] = block.T.astype(BF16)
-
-    cot_s[0:1024, :] = cot_ref[...].astype(F32).reshape(1024, 128)
-    for p in range(4):
-        for y in range(4):
-            cot_out[p, y * 64 : (y + 1) * 64, :] = cot_s[pl.ds(p * 4 + y, 64, stride=16), :].astype(BF16)
 
 
 def layers_kernel(
@@ -228,7 +225,7 @@
     copy.start()
 
     lane = lax.broadcasted_iota(jnp.int32, (32, 128), 1)
-    ones = jnp.ones((8, 512), BF16)
+    ones = jnp.ones((16, 512), BF16)
     all_cells, all_cols = [], []
     q = jnp.dot(
         wt_ref[...],
@@ -350,7 +347,7 @@
     def edges(*refs):
         edges_kernel(space, *refs)
 
-    inputs = [in_hbm(x) for x in (vol, w1, b1.reshape(1, 32), b2.reshape(1, 64), w2, cot)]
+    weights = [in_hbm(x) for x in (w1, b1.reshape(1, 32), b2.reshape(1, 64), w2)]
     message = jax.ShapeDtypeStruct((4 * HALO + 16, 8, 256), BF16)
     to_pair, to_other, split, compact, spread = pl.pallas_call(
         edges,
@@ -366,7 +363,7 @@
         scratch_shapes=[pltpu.VMEM((2, 64, 4, 128), BF16), pltpu.SemaphoreType.DMA((2, 5))],
         compiler_params=pltpu.CompilerParams(vmem_limit_bytes=8 * 2**20),
         name="edges",
-    )(inputs[0], inputs[-1])
+    )(in_hbm(vol), in_hbm(cot))
     pairs = [(i, i ^ 1) for i in range(count)]
     others = [(i, i + 1) for i in range(1, count - 1, 2)] + [(i + 1, i) for i in range(1, count - 1, 2)]
     from_other = lax.ppermute(to_other, space, others)
@@ -385,20 +382,20 @@
     own = pl.pallas_call(
         own_kernel,
         out_shape=tuple(jax.ShapeDtypeStruct(*shape) for shape in shapes),
-        in_specs=[anywhere] * 6 + [vmem] * 2,
+        in_specs=[anywhere] * 4 + [vmem] * 4,
         out_specs=(vmem,) * len(shapes),
         scratch_shapes=[
-            *(pltpu.VMEM(x.shape, x.dtype) for x in inputs),
+            *(pltpu.VMEM(x.shape, x.dtype) for x in weights),
             pltpu.VMEM((16, 128), F32),
             pltpu.VMEM((8 * 128 + 8, 128), F32),
             pltpu.VMEM((1040, 128), F32),
             pltpu.VMEM((64, 1024), F32),
-            pltpu.SemaphoreType.DMA((6,)),
+            pltpu.SemaphoreType.DMA((4,)),
         ],
         compiler_params=pltpu.CompilerParams(vmem_limit_bytes=16 * 2**20),
         cost_estimate=pl.CostEstimate(flops=500_000_000, bytes_accessed=4_000_000, transcendentals=0),
         name="own_planes",
-    )(*inputs, split, spread)
+    )(*weights, vol, cot, split, spread)
 
     def kernel(*refs):
         layers_kernel(

time: 67.8 us -> 67.8 us (level)
  no operation moved by 1% of the time
where the time goes in v6:
time: 67.8 us; the launch traced here: 67.5 us
  blocking collectives  50 us (74%)
  starting transfers between devices  9.46 us (14%)
  Pallas kernels  7.32 us (11%)
  between operations  0.73 us (1%)
    all_to_all x3, blocking collectives, sum_everywhere(): parts = lax.all_to_all(packed, axes, 0, 0, tiled=True)  38.6 us
    all_to_all x1, blocking collectives, sum_everywhere(): return lax.all_to_all(packed, CORES, 0, 0, tiled=True)  11.4 us
    ppermute x1, starting transfers between devices, local_step(): from_pair = lax.ppermute(to_pair, space, pairs)  4.86 us
    ppermute x1, starting transfers between devices, local_step(): from_other = lax.ppermute(to_other, space, others)  4.59 us
    pallas_call x1, Pallas kernels, local_step(): pl.pallas_call(kernel, out_shape=(jax.ShapeDtypeStruct((64, 16, 128), BF1...  3.47 us
    pallas_call x1, Pallas kernels, local_step(): pl.pallas_call(own_kernel, out_shape=tuple((jax.ShapeDtypeStruct(*shape)...  1.88 us
  transfers between devices with their start and end apart: 2, of which 0 were waited for; matrix products, arithmetic and copies ran while one was open for 0% of the time, Pallas kernels for 3%

profile of v6, /device:TPU:1, one launch (start us, length us, event | category | flops | bytes accessed | tf_op | source)
XLA Modules:
  0.0 67.5 jit_solution(5291223278518170354)
XLA Ops:
  0.6 0.0 copy-start
  0.6 0.0 copy-start.1
  0.7 1.1 %edges.1 = (bf16[36,8,256]{2,1,0:T(8,128)(2,1)S(1)}, bf16[36,8,256]{2,1,0:T(8,128)(2,1)S(1)}, bf16[256,512]{1,0:T(8,128)(2,1)S(1)}, f32[256,128]{1,0:T(8,128)S(1)}, bf16[108,256]{1,0:T(8,128)(2,1)S(1)}) custom-call(bf16[4,8,8,256]{3,2,1,0:T(8,128)(2,1)} %bitcast.9, bf16[64,4,4,128]{3,2,1,0:T(4,128)(2,1)} %bitcast.7), custom_call_target="tpu_custom_call" | custom-call | tf_op jit(solution)/shard_map/edges/pallas_call | solution.py:352
  1.8 4.6 %collective-permute-start = (bf16[36,8,256]{2,1,0:T(8,128)(2,1)S(1)}, bf16[36,8,256]{2,1,0:T(8,128)(2,1)S(1)}, u32[]{:S(2)}, u32[]{:S(2)}) collective-permute-start(bf16[36,8,256]{2,1,0:T(8,128)(2,1)S(1)} %get-tuple-element.25), channel_id=1, source_target_pairs={{1,2},{3,4},{5,6},{7,8},{9,10},{11,12},{13,14},{15,16},{17,18},{19... | collective-permute-start | bytes 442376 | tf_op jit(solution)/shard_map/ppermute | solution.py:369
  6.4 4.9 %collective-permute-start.1 = (bf16[36,8,256]{2,1,0:T(8,128)(2,1)S(1)}, bf16[36,8,256]{2,1,0:T(8,128)(2,1)S(1)}, u32[]{:S(2)}, u32[]{:S(2)}) collective-permute-start(bf16[36,8,256]{2,1,0:T(8,128)(2,1)S(1)} %get-tuple-element.26), channel_id=1, source_target_pairs={{0,1},{1,0},{2,3},{3,2},{4,5},{5,4},{6,7},{7,6},{8,9},{9,8},{10,11... | collective-permute-start | bytes 442376 | tf_op jit(solution)/shard_map/ppermute | solution.py:370
  11.3 0.0 copy-done
  11.3 0.0 copy-done.1
  11.3 1.9 %own_planes.1 = (bf16[256,256]{1,0:T(8,128)(2,1)S(1)}, bf16[256,1152]{1,0:T(8,128)(2,1)S(1)}, bf16[384,768]{1,0:T(8,128)(2,1)S(1)}, f32[256,128]{1,0:T(8,128)S(1...) custom-call(bf16[32,108]{1,0:T(8,128)(2,1)} %w1_hbm.1, ...), custom_call_target="tpu_custom_call" | custom-call | flops 500000000 | bytes 4000000 | tf_op jit(solution)/shard_map/own_planes/pallas_call | solution.py:382
  13.2 0.0 collective-permute-done.refs_0_
  13.2 0.0 collective-permute-done.1.refs_1_
  13.2 3.5 %layers.1 = (bf16[64,16,128]{2,1,0:T(8,128)(2,1)}, bf16[8,64,128]{2,1,0:T(8,128)(2,1)S(1)}) custom-call(bf16[36,8,256]{2,1,0:T(8,128)(2,1)S(1)} %collective-permute-done.refs_0_, bf16[36,8,256]{2,1,0:T(8,128)(2,1)S(1)} %collective-permute-done.1.refs_1_, bf16[256,512]{1,0:T(8,128)(2,1)S(1)} %get-tuple-element.27.split_ref.refs_2_, ...), custom_call_target="tpu_custom_call" | custom-call | flops 2500000000 | bytes 4000000 | tf_op jit(solution)/shard_map/layers/pallas_call | solution.py:409
  16.7 9.7 %all_to_all.20.parts_ref = bf16[8,64,128]{2,1,0:T(8,128)(2,1)S(1)} all-to-all(bf16[8,64,128]{2,1,0:T(8,128)(2,1)S(1)} %get-tuple-element.40), channel_id=1, replica_groups=mesh['z2'=2,'z1'=2,'z0'=2,'y2'=2,'x1'=2,'x0'=2,'y1'=2,'y0'=2,'c'=2] {'x0..., dimensions={0} | all-to-all | bytes 262144 | tf_op jit(solution)/shard_map/all_to_all | solution.py:331
  26.4 12.4 %all_to_all.21.parts_ref = bf16[8,64,128]{2,1,0:T(8,128)(2,1)S(1)} all-to-all(bf16[8,64,128]{2,1,0:T(8,128)(2,1)S(1)} %add.3), channel_id=1, replica_groups=mesh['z2'=2,'z1'=2,'z0'=2,'y2'=2,'x1'=2,'x0'=2,'y1'=2,'y0'=2,'c'=2] {'y0..., dimensions={0} | all-to-all | bytes 262144 | tf_op jit(solution)/shard_map/all_to_all | solution.py:331
  38.8 16.6 %all_to_all.22.parts_ref = bf16[8,64,128]{2,1,0:T(8,128)(2,1)S(1)} all-to-all(bf16[8,64,128]{2,1,0:T(8,128)(2,1)S(1)} %add.4), channel_id=1, replica_groups=mesh['z2'=2,'z1'=2,'z0'=2,'y2'=2,'x1'=2,'x0'=2,'y1'=2,'y0'=2,'c'=2] {'z0..., dimensions={0} | all-to-all | bytes 262144 | tf_op jit(solution)/shard_map/all_to_all | solution.py:331
  55.3 11.4 %all_to_all.23.total_ref = bf16[8,64,128]{2,1,0:T(8,128)(2,1)S(1)} all-to-all(bf16[8,64,128]{2,1,0:T(8,128)(2,1)S(1)} %add.5), channel_id=1, replica_groups=mesh['z2'=2,'z1'=2,'z0'=2,'y2'=2,'x1'=2,'x0'=2,'y1'=2,'y0'=2,'c'=2] {'x0..., dimensions={0} | all-to-all | bytes 262144 | tf_op jit(solution)/shard_map/all_to_all | solution.py:340
  66.7 0.8 %unpack.1 = (f32[32,108]{1,0:T(8,128)}, f32[1,32]{1,0:T(1,128)}, f32[64,864]{1,0:T(8,128)}, f32[1,64]{1,0:T(1,128)}) custom-call(bf16[8,64,128]{2,1,0:T(8,128)(2,1)S(1)} %all_to_all.23.total_ref), custom_call_target="tpu_custom_call" | custom-call | tf_op jit(solution)/shard_map/unpack/pallas_call | solution.py:444
  (3 shorter events, 0.1 us)
Async XLA Ops:
  0.6 10.6 %copy-start = (bf16[1,64,4,4,128]{4,3,2,1,0:T(4,128)(2,1)S(1)}, bf16[1,64,4,4,128]{4,3,2,1,0:T(4,128)(2,1)}, u32[]{:S(2)}) copy-start(bf16[1,64,4,4,128]{4,3,2,1,0:T(4,128)(2,1)} %param.11) | copy-start | bytes 786436
  0.6 10.6 %copy-start.1 = (bf16[1,4,8,8,256]{4,3,2,1,0:T(8,128)(2,1)S(1)}, bf16[1,4,8,8,256]{4,3,2,1,0:T(8,128)(2,1)}, u32[]{:S(2)}) copy-start(bf16[1,4,8,8,256]{4,3,2,1,0:T(8,128)(2,1)} %param.6) | copy-start | bytes 393220
  1.8 11.4 %collective-permute-start = (bf16[36,8,256]{2,1,0:T(8,128)(2,1)S(1)}, bf16[36,8,256]{2,1,0:T(8,128)(2,1)S(1)}, u32[]{:S(2)}, u32[]{:S(2)}) collective-permute-start(bf16[36,8,256]{2,1,0:T(8,128)(2,1)S(1)} %get-tuple-element.25), channel_id=1, source_target_pairs={{1,2},{3,4},{5,6},{7,8},{9,10},{11,12},{13,14},{15,16},{17,18},{19... | collective-permute-start | bytes 442376 | tf_op jit(solution)/shard_map/ppermute | solution.py:369
  6.4 6.8 %collective-permute-start.1 = (bf16[36,8,256]{2,1,0:T(8,128)(2,1)S(1)}, bf16[36,8,256]{2,1,0:T(8,128)(2,1)S(1)}, u32[]{:S(2)}, u32[]{:S(2)}) collective-permute-start(bf16[36,8,256]{2,1,0:T(8,128)(2,1)S(1)} %get-tuple-element.26), channel_id=1, source_target_pairs={{0,1},{1,0},{2,3},{3,2},{4,5},{5,4},{6,7},{7,6},{8,9},{9,8},{10,11... | collective-permute-start | bytes 442376 | tf_op jit(solution)/shard_map/ppermute | solution.py:370

commit v7 on v6

--- a/solution.py
+++ b/solution.py
@@ -162,7 +162,7 @@
     other_ref, pair_ref,
     split_ref, compact_ref, w1_ref, wexp_ref, wt_ref, b1_ref, b2_ref, cot_ref, win, pre_own, pooled_own,
     act_ref, grad_ref,
-    fine, win_low, win_high, cot_s, ps, pre_s, g2s, act_s, act_out, sem,
+    fine, win_low, win_high, cot_s, ps, pre_s, g2s, act_s,
     *, space, last, scale_first, scale_second,
 ):
     place = lax.axis_index(space)
@@ -220,9 +220,7 @@
             cot = jnp.concatenate([cot_s[pl.ds(y, 64, stride=4), :] for y in range(4)], axis=0)
         own = pre[:, r * 128 : (r + 1) * 128]
         g2s[r * 256 : (r + 1) * 256, :] = jnp.where(own > 0, cot, leak_slope * cot).astype(BF16)
-    act_out[...] = act_s[0:1024, :].reshape(64, 16, 128).astype(BF16)
-    copy = pltpu.make_async_copy(act_out, act_ref, sem)
-    copy.start()
+    act_ref[...] = act_s[0:1024, :].reshape(64, 16, 128).astype(BF16)
 
     lane = lax.broadcasted_iota(jnp.int32, (32, 128), 1)
     ones = jnp.ones((16, 512), BF16)
@@ -299,20 +297,22 @@
     grad_ref[7, 0:32, :] = (w1_grad * scale_first).astype(BF16)
     grad_ref[7, 32:48, :] = biases.astype(BF16)
     grad_ref[7, 48:64, :] = jnp.zeros((16, 128), BF16)
-    copy.wait()
-
-
-def unpack_kernel(total_ref, w1_ref, b1_ref, w2_ref, b2_ref, w1_s, b1_s, w2_s, b2_s, sems):
+
+
+def finish_kernel(
+    total_ref, act_s, w1_ref, b1_ref, w2_ref, b2_ref, act_ref, w1_s, b1_s, w2_s, b2_s, sems
+):
+    copies = []
+
+    def send(source, target):
+        copies.append(pltpu.make_async_copy(source, target, sems.at[len(copies)]))
+        copies[-1].start()
+
+    send(act_s, act_ref)
     rest = total_ref[7].astype(F32)
     w1_s[...] = rest[0:32, 0:108]
     b1_s[...] = rest[32:33, 0:32]
     b2_s[...] = rest[40:41, 0:64]
-    copies = []
-
-    def send(source, target):
-        copies.append(pltpu.make_async_copy(source, target, sems.at[len(copies)]))
-        copies[-1].start()
-
     send(w1_s, w1_ref)
     send(b1_s, b1_ref)
     send(b2_s, b2_ref)
@@ -413,7 +413,7 @@
             jax.ShapeDtypeStruct((8, 64, 128), BF16),
         ),
         in_specs=[vmem] * (4 + len(shapes)),
-        out_specs=(anywhere, vmem),
+        out_specs=(vmem, vmem),
         scratch_shapes=[
             pltpu.VMEM((2, HALO * 128 + 8, 128), F32),
             pltpu.VMEM((HALO, 160, 128), BF16),
@@ -423,14 +423,12 @@
             pltpu.VMEM((2, 4, 256, 128), BF16),
             pltpu.VMEM((6 * 256, 128), BF16),
             pltpu.VMEM((1040, 128), F32),
-            pltpu.VMEM((64, 16, 128), BF16),
-            pltpu.SemaphoreType.DMA,
         ],
         compiler_params=pltpu.CompilerParams(vmem_limit_bytes=32 * 2**20),
         cost_estimate=pl.CostEstimate(flops=2_500_000_000, bytes_accessed=4_000_000, transcendentals=0),
         name="layers",
     )(from_other, from_pair, split, compact, *own)
-    return act.reshape(1, 64, 4, 4, 128), packed
+    return act, packed
 
 
 def solution(mesh):
@@ -441,27 +439,28 @@
         cells = float(math.prod(volume.shape[2:]) * dp * space)
         act, packed = local_step(volume, w1, b1, w2, b2, cotangent, SPACE, space, cells)
         total = sum_everywhere(packed)
-        gw1, gb1, gw2, gb2 = pl.pallas_call(
-            unpack_kernel,
+        gw1, gb1, gw2, gb2, act = pl.pallas_call(
+            finish_kernel,
             out_shape=(
                 jax.ShapeDtypeStruct((32, 108), F32),
                 jax.ShapeDtypeStruct((1, 32), F32),
                 jax.ShapeDtypeStruct((64, 864), F32),
                 jax.ShapeDtypeStruct((1, 64), F32),
+                jax.ShapeDtypeStruct((64, 16, 128), BF16),
             ),
-            in_specs=[pl.BlockSpec(memory_space=pltpu.VMEM)],
-            out_specs=(pl.BlockSpec(memory_space=pl.ANY),) * 4,
+            in_specs=[pl.BlockSpec(memory_space=pltpu.VMEM)] * 2,
+            out_specs=(pl.BlockSpec(memory_space=pl.ANY),) * 5,
             scratch_shapes=[
                 pltpu.VMEM((32, 108), F32),
                 pltpu.VMEM((1, 32), F32),
                 pltpu.VMEM((64, 864), F32),
                 pltpu.VMEM((1, 64), F32),
-                pltpu.SemaphoreType.DMA((7,)),
+                pltpu.SemaphoreType.DMA((8,)),
             ],
             compiler_params=pltpu.CompilerParams(vmem_limit_bytes=8 * 2**20),
-            name="unpack",
-        )(total)
-        return act, gw1, gb1[0], gw2, gb2[0]
+            name="finish",
+        )(total, act)
+        return act.reshape(1, 64, 4, 4, 128), gw1, gb1[0], gw2, gb2[0]
 
     shared = P(DP, None, SPACE, None, None)
     return jax.shard_map(

time: 67.8 us -> 67.8 us (level)
  no operation moved by 1% of the time
where the time goes in v7:
time: 67.8 us; the launch traced here: 67.5 us
  blocking collectives  50 us (74%)
  starting transfers between devices  9.46 us (14%)
  Pallas kernels  7.3 us (11%)
  between operations  0.72 us (1%)
    all_to_all x3, blocking collectives, sum_everywhere(): parts = lax.all_to_all(packed, axes, 0, 0, tiled=True)  38.6 us
    all_to_all x1, blocking collectives, sum_everywhere(): return lax.all_to_all(packed, CORES, 0, 0, tiled=True)  11.4 us
    ppermute x1, starting transfers between devices, local_step(): from_pair = lax.ppermute(to_pair, space, pairs)  4.86 us
    ppermute x1, starting transfers between devices, local_step(): from_other = lax.ppermute(to_other, space, others)  4.59 us
    pallas_call x1, Pallas kernels, local_step(): pl.pallas_call(kernel, out_shape=(jax.ShapeDtypeStruct((64, 16, 128), BF1...  3.36 us
    pallas_call x1, Pallas kernels, local_step(): pl.pallas_call(own_kernel, out_shape=tuple((jax.ShapeDtypeStruct(*shape)...  1.88 us
  transfers between devices with their start and end apart: 2, of which 0 were waited for; matrix products, arithmetic and copies ran while one was open for 0% of the time, Pallas kernels for 3%

profile of v7, /device:TPU:1, one launch (start us, length us, event | category | flops | bytes accessed | tf_op | source)
XLA Modules:
  0.0 67.5 jit_solution(7546757512721966076)
XLA Ops:
  0.6 0.0 copy-start
  0.6 0.0 copy-start.1
  0.7 1.1 %edges.1 = (bf16[36,8,256]{2,1,0:T(8,128)(2,1)S(1)}, bf16[36,8,256]{2,1,0:T(8,128)(2,1)S(1)}, bf16[256,512]{1,0:T(8,128)(2,1)S(1)}, f32[256,128]{1,0:T(8,128)S(1)}, bf16[108,256]{1,0:T(8,128)(2,1)S(1)}) custom-call(bf16[4,8,8,256]{3,2,1,0:T(8,128)(2,1)} %bitcast.9, bf16[64,4,4,128]{3,2,1,0:T(4,128)(2,1)} %bitcast.7), custom_call_target="tpu_custom_call" | custom-call | tf_op jit(solution)/shard_map/edges/pallas_call | solution.py:352
  1.8 4.6 %collective-permute-start = (bf16[36,8,256]{2,1,0:T(8,128)(2,1)S(1)}, bf16[36,8,256]{2,1,0:T(8,128)(2,1)S(1)}, u32[]{:S(2)}, u32[]{:S(2)}) collective-permute-start(bf16[36,8,256]{2,1,0:T(8,128)(2,1)S(1)} %get-tuple-element.26), channel_id=1, source_target_pairs={{1,2},{3,4},{5,6},{7,8},{9,10},{11,12},{13,14},{15,16},{17,18},{19... | collective-permute-start | bytes 442376 | tf_op jit(solution)/shard_map/ppermute | solution.py:369
  6.4 4.9 %collective-permute-start.1 = (bf16[36,8,256]{2,1,0:T(8,128)(2,1)S(1)}, bf16[36,8,256]{2,1,0:T(8,128)(2,1)S(1)}, u32[]{:S(2)}, u32[]{:S(2)}) collective-permute-start(bf16[36,8,256]{2,1,0:T(8,128)(2,1)S(1)} %get-tuple-element.27), channel_id=1, source_target_pairs={{0,1},{1,0},{2,3},{3,2},{4,5},{5,4},{6,7},{7,6},{8,9},{9,8},{10,11... | collective-permute-start | bytes 442376 | tf_op jit(solution)/shard_map/ppermute | solution.py:370
  11.3 0.0 copy-done
  11.3 0.0 copy-done.1
  11.3 1.9 %own_planes.1 = (bf16[256,256]{1,0:T(8,128)(2,1)S(1)}, bf16[256,1152]{1,0:T(8,128)(2,1)S(1)}, bf16[384,768]{1,0:T(8,128)(2,1)S(1)}, f32[256,128]{1,0:T(8,128)S(1...) custom-call(bf16[32,108]{1,0:T(8,128)(2,1)} %w1_hbm.1, ...), custom_call_target="tpu_custom_call" | custom-call | flops 500000000 | bytes 4000000 | tf_op jit(solution)/shard_map/own_planes/pallas_call | solution.py:382
  13.2 0.0 collective-permute-done.refs_0_
  13.2 0.0 collective-permute-done.1.refs_1_
  13.2 3.4 %layers.1 = (bf16[64,16,128]{2,1,0:T(8,128)(2,1)S(1)}, bf16[8,64,128]{2,1,0:T(8,128)(2,1)S(1)}) custom-call(bf16[36,8,256]{2,1,0:T(8,128)(2,1)S(1)} %collective-permute-done.refs_0_, bf16[36,8,256]{2,1,0:T(8,128)(2,1)S(1)} %collective-permute-done.1.refs_1_, bf16[256,512]{1,0:T(8,128)(2,1)S(1)} %get-tuple-element.28.split_ref.refs_2_, ...), custom_call_target="tpu_custom_call" | custom-call | flops 2500000000 | bytes 4000000 | tf_op jit(solution)/shard_map/layers/pallas_call | solution.py:409
  16.6 9.7 %all_to_all.20.parts_ref = bf16[8,64,128]{2,1,0:T(8,128)(2,1)S(1)} all-to-all(bf16[8,64,128]{2,1,0:T(8,128)(2,1)S(1)} %get-tuple-element.40), channel_id=1, replica_groups=mesh['z2'=2,'z1'=2,'z0'=2,'y2'=2,'x1'=2,'x0'=2,'y1'=2,'y0'=2,'c'=2] {'x0..., dimensions={0} | all-to-all | bytes 262144 | tf_op jit(solution)/shard_map/all_to_all | solution.py:331
  26.2 12.4 %all_to_all.21.parts_ref = bf16[8,64,128]{2,1,0:T(8,128)(2,1)S(1)} all-to-all(bf16[8,64,128]{2,1,0:T(8,128)(2,1)S(1)} %add.3), channel_id=1, replica_groups=mesh['z2'=2,'z1'=2,'z0'=2,'y2'=2,'x1'=2,'x0'=2,'y1'=2,'y0'=2,'c'=2] {'y0..., dimensions={0} | all-to-all | bytes 262144 | tf_op jit(solution)/shard_map/all_to_all | solution.py:331
  38.6 16.6 %all_to_all.22.parts_ref = bf16[8,64,128]{2,1,0:T(8,128)(2,1)S(1)} all-to-all(bf16[8,64,128]{2,1,0:T(8,128)(2,1)S(1)} %add.4), channel_id=1, replica_groups=mesh['z2'=2,'z1'=2,'z0'=2,'y2'=2,'x1'=2,'x0'=2,'y1'=2,'y0'=2,'c'=2] {'z0..., dimensions={0} | all-to-all | bytes 262144 | tf_op jit(solution)/shard_map/all_to_all | solution.py:331
  55.2 11.4 %all_to_all.23.total_ref = bf16[8,64,128]{2,1,0:T(8,128)(2,1)S(1)} all-to-all(bf16[8,64,128]{2,1,0:T(8,128)(2,1)S(1)} %add.5), channel_id=1, replica_groups=mesh['z2'=2,'z1'=2,'z0'=2,'y2'=2,'x1'=2,'x0'=2,'y1'=2,'y0'=2,'c'=2] {'x0..., dimensions={0} | all-to-all | bytes 262144 | tf_op jit(solution)/shard_map/all_to_all | solution.py:340
  66.6 0.8 %finish.1 = (f32[32,108]{1,0:T(8,128)}, f32[1,32]{1,0:T(1,128)}, f32[64,864]{1,0:T(8,128)}, f32[1,64]{1,0:T(1,128)}, bf16[64,16,128]{2,1,0:T(8,128)(2,1)}) custom-call(bf16[8,64,128]{2,1,0:T(8,128)(2,1)S(1)} %all_to_all.23.total_ref, bf16[64,16,128]{2,1,0:T(8,128)(2,1)S(1)} %get-tuple-element.41.act_s), custom_call_target="tpu_custom_call" | custom-call | tf_op jit(solution)/shard_map/finish/pallas_call | solution.py:442
  (3 shorter events, 0.1 us)
Async XLA Ops:
  0.6 10.6 %copy-start = (bf16[1,64,4,4,128]{4,3,2,1,0:T(4,128)(2,1)S(1)}, bf16[1,64,4,4,128]{4,3,2,1,0:T(4,128)(2,1)}, u32[]{:S(2)}) copy-start(bf16[1,64,4,4,128]{4,3,2,1,0:T(4,128)(2,1)} %param.11) | copy-start | bytes 786436
  0.6 10.6 %copy-start.1 = (bf16[1,4,8,8,256]{4,3,2,1,0:T(8,128)(2,1)S(1)}, bf16[1,4,8,8,256]{4,3,2,1,0:T(8,128)(2,1)}, u32[]{:S(2)}) copy-start(bf16[1,4,8,8,256]{4,3,2,1,0:T(8,128)(2,1)} %param.6) | copy-start | bytes 393220
  1.8 11.4 %collective-permute-start = (bf16[36,8,256]{2,1,0:T(8,128)(2,1)S(1)}, bf16[36,8,256]{2,1,0:T(8,128)(2,1)S(1)}, u32[]{:S(2)}, u32[]{:S(2)}) collective-permute-start(bf16[36,8,256]{2,1,0:T(8,128)(2,1)S(1)} %get-tuple-element.26), channel_id=1, source_target_pairs={{1,2},{3,4},{5,6},{7,8},{9,10},{11,12},{13,14},{15,16},{17,18},{19... | collective-permute-start | bytes 442376 | tf_op jit(solution)/shard_map/ppermute | solution.py:369
  6.4 6.8 %collective-permute-start.1 = (bf16[36,8,256]{2,1,0:T(8,128)(2,1)S(1)}, bf16[36,8,256]{2,1,0:T(8,128)(2,1)S(1)}, u32[]{:S(2)}, u32[]{:S(2)}) collective-permute-start(bf16[36,8,256]{2,1,0:T(8,128)(2,1)S(1)} %get-tuple-element.27), channel_id=1, source_target_pairs={{0,1},{1,0},{2,3},{3,2},{4,5},{5,4},{6,7},{7,6},{8,9},{9,8},{10,11... | collective-permute-start | bytes 442376 | tf_op jit(solution)/shard_map/ppermute | solution.py:370
